TPU v7x, 32 devices: a whole 2x2x4 slice. The times are simulated.
32 devices in a mesh: fsdp: 16 (over z, x, core), tp: 2 (over y).
Axes of the slice: x: 2, y: 2, z: 4, core: 2. Of those that a mesh axis runs over, the one named last changes fastest.
Arguments:
- tokens: bfloat16 [8192, 2048], P(('fsdp', 'tp')), may hold values from -6 to 6
- cotangent: bfloat16 [8192, 2048], P(('fsdp', 'tp')), may hold values from -6 to 6
- valid_len: int32 [16], replicated, may hold values from 256 to 512, as said below
- pic_start: int32 [16], replicated, may hold values from 0 to 256, as said below
- norm_gains: float32 [2, 2048], replicated, may hold values from 0.5 to 1.5
- norm_moment: float32 [2, 2048], replicated, may hold values from -96 to 96
- norm_square: float32 [2, 2048], replicated, may hold values from 18.0224 to 73.728
- head_gains: float32 [2, 128], replicated, may hold values from 0.5 to 1.5
- head_moment: float32 [2, 128], replicated, may hold values from -448 to 448
- head_square: float32 [2, 128], replicated, may hold values from 409.6 to 1638.4
- query_weight: float32 [2048, 2048], P('fsdp', 'tp'), may hold values from -0.125 to 0.125
- query_moment: float32 [2048, 2048], P('fsdp', 'tp'), may hold values from -112 to 112
- query_square: float32 [2048, 2048], P('fsdp', 'tp'), may hold values from 24.576 to 106.496
- keyvalue_matrix: float32 [2, 2048, 1024], P(None, 'fsdp', 'tp'), may hold values from -0.125 to 0.125
- keyvalue_first_moment: float32 [2, 2048, 1024], P(None, 'fsdp', 'tp'), may hold values from -96 to 96
- keyvalue_second_moment: float32 [2, 2048, 1024], P(None, 'fsdp', 'tp'), may hold values from 20.48 to 81.92
- headgate_weight: float32 [2048, 16], P('fsdp', 'tp'), may hold values from -0.125 to 0.125
- headgate_moment: float32 [2048, 16], P('fsdp', 'tp'), may hold values from -256 to 256
- headgate_square: float32 [2048, 16], P('fsdp', 'tp'), may hold values from 163.84 to 696.32
- output_weight: float32 [2048, 2048], P('tp', 'fsdp'), may hold values from -1.5 to 1.5
- output_moment: float32 [2048, 2048], P('tp', 'fsdp'), may hold values from -6 to 6
- output_square: float32 [2048, 2048], P('tp', 'fsdp'), may hold values from 0.08192 to 0.32768
- gateup_weight: float32 [2, 2048, 6144], P(None, 'fsdp', 'tp'), may hold values from -0.125 to 0.125
- gateup_moment: float32 [2, 2048, 6144], P(None, 'fsdp', 'tp'), may hold values from -20 to 20
- gateup_square: float32 [2, 2048, 6144], P(None, 'fsdp', 'tp'), may hold values from 0.8192 to 3.2768
- down_weight: float32 [6144, 2048], P('tp', 'fsdp'), may hold values from -0.078125 to 0.078125
- down_moment: float32 [6144, 2048], P('tp', 'fsdp'), may hold values from -32 to 32
- down_square: float32 [6144, 2048], P('tp', 'fsdp'), may hold values from 2.94912 to 11.4688
Outputs:
- block_output: bfloat16 [8192, 2048], P(('fsdp', 'tp'))
- tokens_grad: float32 [8192, 2048], P(('fsdp', 'tp'))
- branch_scales: float32 [3], replicated
- updated_norms: float32 [2, 2048], replicated
- momentum_norms: float32 [2, 2048], replicated
- variance_norms: float32 [2, 2048], replicated
- updated_heads: float32 [2, 128], replicated
- momentum_heads: float32 [2, 128], replicated
- variance_heads: float32 [2, 128], replicated
- updated_query: float32 [2048, 2048], P('fsdp', 'tp')
- momentum_query: float32 [2048, 2048], P('fsdp', 'tp')
- variance_query: float32 [2048, 2048], P('fsdp', 'tp')
- updated_keyvalue: float32 [2, 2048, 1024], P(None, 'fsdp', 'tp')
- momentum_keyvalue: float32 [2, 2048, 1024], P(None, 'fsdp', 'tp')
- variance_keyvalue: float32 [2, 2048, 1024], P(None, 'fsdp', 'tp')
- updated_headgate: float32 [2048, 16], P('fsdp', 'tp')
- momentum_headgate: float32 [2048, 16], P('fsdp', 'tp')
- variance_headgate: float32 [2048, 16], P('fsdp', 'tp')
- updated_output: float32 [2048, 2048], P('tp', 'fsdp')
- momentum_output: float32 [2048, 2048], P('tp', 'fsdp')
- variance_output: float32 [2048, 2048], P('tp', 'fsdp')
- updated_gateup: float32 [2, 2048, 6144], P(None, 'fsdp', 'tp')
- momentum_gateup: float32 [2, 2048, 6144], P(None, 'fsdp', 'tp')
- variance_gateup: float32 [2, 2048, 6144], P(None, 'fsdp', 'tp')
- updated_down: float32 [6144, 2048], P('tp', 'fsdp')
- momentum_down: float32 [6144, 2048], P('tp', 'fsdp')
- variance_down: float32 [6144, 2048], P('tp', 'fsdp')
Inputs may be any that keep to these rules, and one draw needn't show every extreme that they name: The first valid_len[s] tokens of sequence s are valid, the rest are padding; some sequence has all 512 tokens valid. Sequence s holds one picture piece of 256 tokens from pic_start[s], with pic_start[s] + 256 <= valid_len[s].
All inputs are finite; a program needn't handle non-finite values.
Results may differ from a plain program's by a relative error of at most 0.012.
Values may be sent and summed in bfloat16 or wider, within the bound.
A program may use at most 384 MiB of HBM per device.

v0:
```python
import jax
import jax.numpy as jnp
from jax import lax
from jax.experimental import pallas as pl
from jax.experimental.pallas import tpu as pltpu
from jax.sharding import Mesh
from jax.sharding import PartitionSpec as P

MODEL_WIDTH = 2048
QUERY_HEADS = 16
HEAD_WIDTH = 128
FF = 6144
PIC = 256
STEP = 10

norm_epsilon = 1e-06
rope_base = 1000000.0
beta_first = 0.9
beta_second = 0.999
adam_epsilon = 1e-08
weight_decay = 0.1
masked_score = -1e30
low = jnp.bfloat16
wide = jnp.float32


def normalize(values, scaling):
    return (
        values
        * lax.rsqrt(jnp.mean(values * values, axis=-1, keepdims=True) + norm_epsilon)
        * scaling
    )


def norm_back(values, scaling, upstream):
    factor = lax.rsqrt(jnp.mean(values * values, axis=-1, keepdims=True) + norm_epsilon)
    weighted = upstream * scaling
    projected = jnp.mean(weighted * values, axis=-1, keepdims=True)
    result = factor * weighted - values * (factor * factor * factor) * projected
    return (result, jnp.sum(upstream * values * factor, axis=tuple(range(values.ndim - 1))))


def rotary_tables(length_value):
    halves = HEAD_WIDTH // 2
    frequency = rope_base ** (-(jnp.arange(halves, dtype=wide) * 2.0 / HEAD_WIDTH))
    angles = jnp.arange(length_value, dtype=wide)[:, None] * frequency[None, :]
    cosine, sine = jnp.cos(angles), jnp.sin(angles)
    return (
        jnp.concatenate([cosine, cosine], axis=1),
        jnp.concatenate([-sine, sine], axis=1),
    )


def adam_update(weight, moment, square, gradient, step_rate, decay_rate):
    moment_new = beta_first * moment + (1.0 - beta_first) * gradient
    square_new = beta_second * square + (1.0 - beta_second) * gradient * gradient
    bias_first = 1.0 - beta_first**STEP
    bias_second = 1.0 - beta_second**STEP
    update = moment_new / bias_first / (jnp.sqrt(square_new / bias_second) + adam_epsilon)
    return (weight - step_rate * (update + decay_rate * weight), moment_new, square_new)


def dot(left, right, left_dim, right_dim):
    return lax.dot_general(
        left, right, (((left_dim,), (right_dim,)), ((), ())), preferred_element_type=wide
    )


def fetch(parts):
    pieces = []
    for core in range(2):
        for part in parts:
            size = part.shape[1] // 2
            pieces.append(part[:, core * size : (core + 1) * size].astype(low))
    count = len(parts)
    local_block = jnp.stack(
        [jnp.concatenate(pieces[core * count : (core + 1) * count], axis=1) for core in range(2)]
    )
    return lax.all_gather(local_block, ("w", "c"), axis=1, tiled=True)


def columns_of(both, start, size):
    return lax.dynamic_slice(
        both, (lax.axis_index("c"), 0, start), (1, both.shape[1], size)
    ).reshape(both.shape[1], size)


MESH = pl.DeviceIdType.MESH
BLOCKS = 4
STRIP = 16
ANY = pl.BlockSpec(memory_space=pl.ANY)
VMEM = pl.BlockSpec(memory_space=pltpu.VMEM)


def ring_place(index, count):
    odd = lax.rem(index, 2)
    pair = lax.div(index, 2)
    return (1 - odd) * pair + odd * (count - 1 - pair)


def ring_index(place, count):
    late = lax.div(place, count // 2)
    return (1 - late) * 2 * place + late * (2 * (count - 1 - place) + 1)


class Device:
    def __init__(self, semaphores):
        self.w, self.c, self.t = (lax.axis_index(axis) for axis in ("w", "c", "t"))
        self.count = lax.axis_size("w")
        self.place = ring_place(self.w, self.count)
        self.semaphores = semaphores
        self.used = 0
        self.other_core = {"c": 1 - self.c}
        self.other_row = {"t": 1 - self.t}

    def owner(self, distance):
        return ring_index(lax.rem(self.place + distance + self.count, self.count), self.count)

    def meet(self, partners):
        barrier = pltpu.get_barrier_semaphore()
        for partner in partners:
            pl.semaphore_signal(barrier, inc=1, device_id=partner, device_id_type=MESH)
        pl.semaphore_wait(barrier, len(partners))

    def remote(self, source, target, device):
        slot = self.used
        self.used += 1
        return pltpu.make_async_remote_copy(
            src_ref=source,
            dst_ref=target,
            send_sem=self.semaphores.at[0, slot],
            recv_sem=self.semaphores.at[1, slot],
            device_id=device,
            device_id_type=MESH,
        )

    def inside(self, source, target):
        slot = self.used
        self.used += 1
        return pltpu.make_async_copy(source, target, self.semaphores.at[0, slot])


def rows_at(start, size):
    return pl.ds(pl.multiple_of(start, STRIP), size)


class Spread:
    def __init__(self, device, full):
        self.device, self.full = device, full
        self.size = full.shape[0] // 4
        self.block = self.size // BLOCKS
        self.rows, self.core, self.passed, self.kept = {}, {}, {}, {}

    def where(self, core, row, index):
        return self.full.at[
            rows_at((core * 2 + row) * self.size + index * self.block, self.block)
        ]

    def put(self, index, source):
        device = self.device
        target = self.where(device.c, device.t, index)
        self.rows[index] = device.remote(source, target, device.other_row)
        self.core[index] = device.remote(source, target, device.other_core)
        self.kept[index] = device.inside(source, target)
        for copy in (self.rows[index], self.core[index], self.kept[index]):
            copy.start()

    def forward(self, index):
        device = self.device
        self.rows[index].wait_recv()
        place = self.where(device.c, 1 - device.t, index)
        self.passed[index] = device.remote(place, place, device.other_core)
        self.passed[index].start()

    def finish(self):
        for index in range(BLOCKS):
            self.rows[index].wait_send()
            self.core[index].wait()
            self.passed[index].wait()
            self.kept[index].wait()


class Collect:
    def __init__(self, device, partial, near, far, sent, came):
        self.device = device
        self.partial, self.near, self.far, self.sent, self.came = partial, near, far, sent, came
        self.size = partial.shape[0] // 4
        self.block = self.size // BLOCKS
        self.core, self.rows = {}, {}

    def start(self):
        device = self.device
        self.load = device.inside(
            self.partial.at[rows_at(device.c * 2 * self.size, 2 * self.size)], self.near
        )
        for part, row in enumerate((1 - device.t, device.t)):
            for index in range(BLOCKS):
                start = row * self.size + index * self.block
                copy = device.remote(
                    self.partial.at[rows_at((1 - device.c) * 2 * self.size + start, self.block)],
                    self.far.at[rows_at(start, self.block)],
                    device.other_core,
                )
                copy.start()
                self.core[part, index] = copy
        self.load.start()

    def pass_on(self, index):
        device = self.device
        if index == 0:
            self.load.wait()
        self.core[0, index].wait_recv()

        @pl.loop(0, self.block // STRIP)
        def _(strip):
            at = index * self.block + strip * STRIP
            rows = rows_at((1 - device.t) * self.size + at, STRIP)
            total = self.near[rows, :].astype(wide) + self.far[rows, :].astype(wide)
            self.sent[rows_at(at, STRIP), :] = total.astype(low)

        place = rows_at(index * self.block, self.block)
        self.rows[index] = device.remote(
            self.sent.at[place], self.came.at[place], device.other_row
        )
        self.rows[index].start()

    def take(self, index, use):
        device = self.device
        self.core[1, index].wait_recv()
        self.rows[index].wait_recv()

        @pl.loop(0, self.block // STRIP)
        def _(strip):
            at = index * self.block + strip * STRIP
            rows = rows_at(device.t * self.size + at, STRIP)
            mine = rows_at(at, STRIP)
            total = (
                self.near[rows, :].astype(wide)
                + self.far[rows, :].astype(wide)
                + self.came[mine, :].astype(wide)
            )
            use(mine, total)

    def finish(self):
        for index in range(BLOCKS):
            self.core[0, index].wait_send()
            self.core[1, index].wait_send()
            self.rows[index].wait_send()


class Given:
    parts = 2

    def __init__(self, grads):
        self.rows, self.columns = grads.shape
        self.grads = grads

    def take(self, starts, size):
        return [self.grads[rows_at(start, size), :].astype(wide) for start in starts]

    def sources(self, starts, size, keep):
        return [self.grads.at[rows_at(start, size)] for start in starts]


class Product:
    parts = 1

    def __init__(self, left, right, start, columns):
        self.rows, self.columns = left.shape[1], columns
        self.left, self.right, self.start = left, right, start

    def take(self, starts, size):
        left = jnp.concatenate(
            [self.left[:, pl.ds(pl.multiple_of(start, 128), size)] for start in starts], axis=1
        )
        both = dot(left, self.right[:, self.start : self.start + self.columns], 0, 0)
        return [both[:size], both[size:]]

    def sources(self, starts, size, keep):
        for way, value in enumerate(self.take(starts, size)):
            keep[way] = value.astype(low)
        return [keep.at[way] for way in range(2)]


class RingSum:
    def __init__(self, device, grads, scratch, sums):
        self.device, self.grads, self.sums = device, grads, sums
        self.slots, self.totals, self.first = scratch
        self.half = grads.rows // device.count // 2
        self.parts = grads.parts
        self.part = self.half // self.parts
        self.copies = {}
        self.ticks = [
            (step, part) for step in range(device.count) for part in range(self.parts)
        ]

    def own(self, way, distance, part):
        owner = self.device.owner(-(1 - 2 * way) * distance)
        return (owner * 2 + way) * self.half + part * self.part

    def slot(self, way, step, part):
        return self.slots.at[
            way * (self.device.count - 1) + step, pl.ds(part * self.part, self.part)
        ]

    def send(self, way, step, part, source):
        device = self.device
        copy = device.remote(
            source, self.slot(way, step, part), {"w": device.owner(1 - 2 * way)}
        )
        copy.start()
        self.copies[way, step, part] = copy

    def tick(self, count=1):
        device = self.device
        for _ in range(count):
            if not self.ticks:
                return
            step, part = self.ticks.pop(0)
            starts = [self.own(way, step + 1, part) for way in range(2)]
            if step == 0:
                sources = self.grads.sources(starts, self.part, self.first)
                for way in range(2):
                    self.send(way, step, part, sources[way])
                continue
            own = self.grads.take(starts, self.part)
            for way in range(2):
                self.copies[way, step - 1, part].wait_recv()
                slot = self.slot(way, step - 1, part)
                total = (slot[...].astype(wide) + own[way]).astype(low)
                if step < device.count - 1:
                    slot[...] = total
                    self.send(way, step, part, slot)
                else:
                    self.totals[way, pl.ds(part * self.part, self.part), :] = total

    def close(self):
        device = self.device
        self.tick(len(self.ticks))
        self.away = device.remote(
            self.totals.at[1 - device.c], self.sums.at[device.c], device.other_core
        )
        self.kept = device.inside(self.totals.at[device.c], self.sums.at[device.c])
        self.away.start()
        self.kept.start()

    def finish(self):
        for copy in self.copies.values():
            copy.wait_send()
        self.away.wait()
        self.kept.wait()


def ring_shapes(columns, count):
    half = MODEL_WIDTH // count // 2
    return [
        pltpu.VMEM((2 * (count - 1), half, columns), low),
        pltpu.VMEM((2, half, columns), low),
        pltpu.VMEM((2, half, columns), low),
    ]


class RingWork:
    def __init__(self, pairs):
        self.pairs = pairs
        self.columns = [columns for _, _, _, columns in pairs]
        self.fit = (MODEL_WIDTH // lax.axis_size("w") // 2) % 128 == 0
        self.operands, self.places = [], []
        for left, right, start, columns in pairs:
            if self.fit:
                self.places.append((self.add(left), self.add(right), start, columns))
            else:
                part = right[:, start : start + columns]
                self.places.append((self.add(dot(left, part, 0, 0).astype(low)),))

    def add(self, value):
        for index, other in enumerate(self.operands):
            if other is value:
                return index
        self.operands.append(value)
        return len(self.operands) - 1

    def sources(self, refs):
        sources = [
            Product(refs[place[0]], refs[place[1]], *place[2:]) if self.fit else Given(refs[place[0]])
            for place in self.places
        ]
        return sources, refs[len(self.operands) :]

    def outputs(self):
        half = MODEL_WIDTH // lax.axis_size("w") // 2
        return [jax.ShapeDtypeStruct((2, half, size), low) for size in self.columns]

    def scratch(self):
        count = lax.axis_size("w")
        return [shape for size in self.columns for shape in ring_shapes(size, count)]

    def semaphores(self):
        return 4 * (lax.axis_size("w") + 1) * len(self.columns)


def collect_shapes(size):
    return [
        pltpu.VMEM((2 * size, MODEL_WIDTH), low),
        pltpu.VMEM((2 * size, MODEL_WIDTH), low),
        pltpu.VMEM((size, MODEL_WIDTH), low),
        pltpu.VMEM((size, MODEL_WIDTH), low),
    ]


def semaphores_for(count):
    return pltpu.SemaphoreType.DMA((2, count))


def settings(collective):
    return pltpu.CompilerParams(
        collective_id=collective, has_side_effects=True, vmem_limit_bytes=56 * 2**20
    )


def neighbours(device):
    return [
        device.other_core,
        device.other_row,
        {"w": device.owner(1)},
        {"w": device.owner(-1)},
    ]


class RingGather:
    def __init__(self, device, mine, other, full):
        self.device, self.full = device, full
        self.size = mine.shape[0]
        self.parts = min(4, self.size // STRIP)
        self.part = self.size // self.parts
        here = rows_at((device.w * 2 + device.c) * self.size, self.size)
        self.kept = device.inside(mine, full.at[here])
        self.crossed = device.remote(other, full.at[here], device.other_core)
        self.copies = {}
        self.ticks = [
            (step, part) for step in range(device.count - 1) for part in range(self.parts)
        ]

    def start(self):
        self.kept.start()
        self.crossed.start()

    def ready(self):
        self.kept.wait()
        self.crossed.wait()

    def tick(self, count=1):
        device = self.device
        for _ in range(count):
            if not self.ticks:
                return
            step, part = self.ticks.pop(0)
            for way in range(2):
                if step > 0:
                    self.copies[way, step - 1, part].wait_recv()
                owner = device.owner(-(1 - 2 * way) * step)
                block = self.full.at[
                    rows_at((owner * 2 + way) * self.size + part * self.part, self.part)
                ]
                copy = device.remote(block, block, {"w": device.owner(1 - 2 * way)})
                copy.start()
                self.copies[way, step, part] = copy

    def finish(self):
        self.tick(len(self.ticks))
        for part in range(self.parts):
            for way in range(2):
                self.copies[way, self.device.count - 2, part].wait_recv()
        for copy in self.copies.values():
            copy.wait_send()


def gather_kernel(mine, other, first, second, full, first_full, second_full, semaphores):
    device = Device(semaphores)
    device.meet(neighbours(device))
    gather = RingGather(device, mine, other, full)
    gather.start()
    spreads = []
    for rows, target in ((first, first_full), (second, second_full)):
        spread = Spread(device, target)
        block = spread.block
        for index in range(BLOCKS):
            spread.put(index, rows.at[pl.ds(index * block, block)])
        spreads.append(spread)
    gather.ready()
    for spread in spreads:
        for index in range(BLOCKS):
            gather.tick(gather.parts)
            spread.forward(index)
    gather.finish()
    for spread in spreads:
        spread.finish()


def gather_attention(mine, other, first, second):
    count = lax.axis_size("w")
    rows = first.shape[0] * 4
    return pl.pallas_call(
        gather_kernel,
        out_shape=[
            jax.ShapeDtypeStruct((MODEL_WIDTH, mine.shape[1]), low),
            jax.ShapeDtypeStruct((rows, MODEL_WIDTH), low),
            jax.ShapeDtypeStruct((rows, MODEL_WIDTH), low),
        ],
        in_specs=[ANY] * 4,
        out_specs=[ANY] * 3,
        scratch_shapes=[semaphores_for(8 * count + 8 * BLOCKS + 2)],
        compiler_params=settings(1),
        cost_estimate=pl.CostEstimate(flops=0, bytes_accessed=64 * 2**20, transcendentals=0),
        name="gather_attention",
    )(mine, other, first, second)


def forward_kernel(
    partial, rows, gain, total, full, near, far, sent, came, normed, semaphores
):
    device = Device(semaphores)
    device.meet([device.other_core, device.other_row])
    collect = Collect(device, partial, near, far, sent, came)
    spread = Spread(device, full)
    collect.start()
    for index in range(BLOCKS):
        collect.pass_on(index)

    def use(at, value):
        total[at, :] = value
        middle = rows[at, :].astype(wide) + value
        normed[at, :] = normalize(middle, gain[...]).astype(low)

    for index in range(BLOCKS):
        collect.take(index, use)
        spread.put(index, normed.at[pl.ds(index * spread.block, spread.block)])
    for index in range(BLOCKS):
        spread.forward(index)
    spread.finish()
    collect.finish()


def exchange_forward(partial, rows, gain):
    size = rows.shape[0]
    return pl.pallas_call(
        forward_kernel,
        out_shape=[
            jax.ShapeDtypeStruct((size, MODEL_WIDTH), wide),
            jax.ShapeDtypeStruct((4 * size, MODEL_WIDTH), low),
        ],
        in_specs=[ANY, VMEM, VMEM],
        out_specs=[VMEM, ANY],
        scratch_shapes=collect_shapes(size)
        + [pltpu.VMEM((size, MODEL_WIDTH), low), semaphores_for(16 * BLOCKS)],
        compiler_params=settings(2),
        cost_estimate=pl.CostEstimate(flops=0, bytes_accessed=64 * 2**20, transcendentals=0),
        name="exchange_forward",
    )(partial, rows, gain)


class Rings:
    def __init__(self, rings):
        self.rings = rings
        self.next = 0

    def tick(self, count=1):
        for _ in range(count):
            ring = self.rings[self.next]
            self.next = (self.next + 1) % len(self.rings)
            ring.tick()

    def finish(self):
        while any(ring.ticks for ring in self.rings):
            self.tick()
        for ring in self.rings:
            ring.close()
        for ring in self.rings:
            ring.finish()


def norm_back_rows(values, gain, upstream):
    factor = lax.rsqrt(jnp.mean(values * values, axis=-1, keepdims=True) + norm_epsilon)
    weighted = upstream * gain
    projected = jnp.mean(weighted * values, axis=-1, keepdims=True)
    result = factor * weighted - values * (factor * factor * factor) * projected
    return result, jnp.sum(upstream * values * factor, axis=0, keepdims=True)


def backward_kernel(work, partial, output, middle, rows, gain, counted, *refs):
    count = len(work.columns)
    grads, refs = work.sources(refs)
    grad, gain_grad, output_total, squares, full, refs = *refs[:5], refs[5:]
    sums, refs = refs[:count], refs[count:]
    rounded = refs[8]
    device = Device(refs[-1])
    device.meet(neighbours(device))
    collect = Collect(device, partial, *refs[:4])
    output_collect = Collect(device, output, *refs[4:8])
    spread = Spread(device, full)
    rings = Rings(
        [RingSum(device, grads[i], refs[9 + 3 * i : 12 + 3 * i], sums[i]) for i in range(count)]
    )
    collect.start()
    rings.tick(2)
    gain_grad[...] = jnp.zeros_like(gain_grad)
    squares[...] = jnp.zeros_like(squares)
    for index in range(BLOCKS):
        collect.pass_on(index)
    rings.tick(count - 2)
    output_collect.start()

    def use(at, upstream):
        result, gained = norm_back_rows(middle[at, :], gain[...], upstream)
        result = result + rows[at, :].astype(wide)
        grad[at, :] = result
        rounded[at, :] = result.astype(low)
        gain_grad[...] += gained

    def use_output(at, value):
        output_total[at, :] = value
        squares[...] += jnp.sum(counted[at, :] * value * value, axis=0, keepdims=True)

    for index in range(BLOCKS):
        collect.take(index, use)
        spread.put(index, rounded.at[pl.ds(index * spread.block, spread.block)])
        rings.tick(1)
    for index in range(BLOCKS):
        output_collect.pass_on(index)
    rings.tick(2)
    for index in range(BLOCKS):
        spread.forward(index)
        rings.tick(1)
    for index in range(BLOCKS):
        output_collect.take(index, use_output)
        rings.tick(1)
    rings.finish()
    spread.finish()
    collect.finish()
    output_collect.finish()


def exchange_backward(partial, output, middle, rows, gain, counted, pairs):
    size = rows.shape[0]
    work = RingWork(pairs)

    def body(*refs):
        backward_kernel(work, *refs)

    return pl.pallas_call(
        body,
        out_shape=[
            jax.ShapeDtypeStruct((size, MODEL_WIDTH), wide),
            jax.ShapeDtypeStruct((1, MODEL_WIDTH), wide),
            jax.ShapeDtypeStruct((size, MODEL_WIDTH), wide),
            jax.ShapeDtypeStruct((1, MODEL_WIDTH), wide),
            jax.ShapeDtypeStruct((4 * size, MODEL_WIDTH), low),
            *work.outputs(),
        ],
        in_specs=[ANY, ANY] + [VMEM] * (4 + len(work.operands)),
        out_specs=[VMEM] * 4 + [ANY] * (1 + len(work.columns)),
        scratch_shapes=collect_shapes(size) * 2
        + [pltpu.VMEM((size, MODEL_WIDTH), low)]
        + work.scratch()
        + [semaphores_for(32 * BLOCKS + work.semaphores())],
        compiler_params=settings(3),
        cost_estimate=pl.CostEstimate(flops=0, bytes_accessed=128 * 2**20, transcendentals=0),
        name="exchange_backward",
    )(partial, output, middle, rows, gain, counted, *work.operands)


class Total:
    def __init__(self, device, mine, crossed, gathered):
        self.device, self.mine = device, mine
        self.crossed, self.gathered = crossed, gathered
        self.copies = {}
        self.steps = [("c", 0), ("t", 0)] + [("w", step) for step in range(device.count // 2)]

    def tick(self):
        device = self.device
        if not self.steps:
            return
        axis, step = self.steps.pop(0)
        if axis != "w":
            slot = 0 if axis == "c" else 1
            partner = device.other_core if axis == "c" else device.other_row
            copy = device.remote(self.mine.at[slot], self.crossed.at[slot], partner)
            copy.start()
            copy.wait()
            total = self.mine[slot] + self.crossed[slot]
            if slot == 0:
                self.mine[1] = total
            else:
                self.gathered[device.w] = total
            return
        for way in range(2):
            if way == 1 and step == device.count // 2 - 1:
                continue
            if step > 0:
                self.copies[way, step - 1].wait_recv()
            block = self.gathered.at[device.owner(-(1 - 2 * way) * step)]
            copy = device.remote(block, block, {"w": device.owner(1 - 2 * way)})
            copy.start()
            self.copies[way, step] = copy

    def finish(self, target):
        while self.steps:
            self.tick()
        half = self.device.count // 2
        self.copies[0, half - 1].wait_recv()
        self.copies[1, half - 2].wait_recv()
        for copy in self.copies.values():
            copy.wait_send()
        target[...] = self.gathered[0]
        for index in range(1, self.device.count):
            target[...] += self.gathered[index]


def last_kernel(work, first, tokens, gain, middle_grad, stats, *refs):
    count = len(work.columns)
    grads, refs = work.sources(refs)
    first_total, stats_total, refs = refs[0], refs[1], refs[2:]
    sums, scratch = refs[:count], refs[count:]
    device = Device(scratch[-1])
    device.meet(neighbours(device))
    collect = Collect(device, first, *scratch[:4])
    mine, crossed, gathered = scratch[4:7]
    rings = Rings(
        [
            RingSum(device, grads[i], scratch[7 + 3 * i : 10 + 3 * i], sums[i])
            for i in range(count)
        ]
    )
    total = Total(device, mine, crossed, gathered)
    mine[0] = stats[...]
    collect.start()
    rings.tick(2)
    for index in range(BLOCKS):
        collect.pass_on(index)
    rings.tick(count - 2)

    def use(at, upstream):
        result, gained = norm_back_rows(tokens[at, :].astype(wide), gain[...], upstream)
        first_total[at, :] = result + middle_grad[at, :]
        mine[0, 0:1, :] += gained

    for index in range(BLOCKS):
        collect.take(index, use)
        rings.tick(1)
    while total.steps:
        total.tick()
        rings.tick(1)
    rings.finish()
    total.finish(stats_total)
    collect.finish()


def exchange_last(first, tokens, gain, middle_grad, stats, pairs):
    size = tokens.shape[0]
    count = lax.axis_size("w")
    work = RingWork(pairs)

    def body(*refs):
        last_kernel(work, *refs)

    return pl.pallas_call(
        body,
        out_shape=[
            jax.ShapeDtypeStruct((size, MODEL_WIDTH), wide),
            jax.ShapeDtypeStruct(stats.shape, wide),
            *work.outputs(),
        ],
        in_specs=[ANY] + [VMEM] * (4 + len(work.operands)),
        out_specs=[VMEM] * 2 + [ANY] * len(work.columns),
        scratch_shapes=collect_shapes(size)
        + [
            pltpu.VMEM((2, *stats.shape), wide),
            pltpu.VMEM((2, *stats.shape), wide),
            pltpu.VMEM((count, *stats.shape), wide),
        ]
        + work.scratch()
        + [semaphores_for(16 * BLOCKS + 2 * count + 4 + work.semaphores())],
        compiler_params=settings(4),
        cost_estimate=pl.CostEstimate(flops=0, bytes_accessed=128 * 2**20, transcendentals=0),
        name="exchange_last",
    )(first, tokens, gain, middle_grad, stats, *work.operands)


FEEDFORWARD_ROWS = 256
FEEDFORWARD_COLUMNS = 512


def feedforward_kernel(core, rows, upstream, weights, *refs):
    before, refs = refs[:-5], refs[-5:]
    gate_out, up_out, hidden_out, back_out, down_out = refs
    weight = weights.at[0]
    size = gate_out.shape[1]
    for start in range(0, size, FEEDFORWARD_COLUMNS):
        width = min(FEEDFORWARD_COLUMNS, size - start)
        columns = slice(start, start + width)
        gate_part = dot(rows[...], weight[:, start : start + width], 1, 0)
        up_part = dot(rows[...], weight[:, size + start : size + start + width], 1, 0)
        hidden_grad = dot(
            upstream[...], weight[:, 2 * size + start : 2 * size + start + width], 1, 0
        )
        sigmoid_gate = jax.nn.sigmoid(gate_part)
        silu_gate = gate_part * sigmoid_gate
        hidden_out[:, columns] = (silu_gate * up_part).astype(low)
        gate_out[:, columns] = (
            hidden_grad * up_part * sigmoid_gate * (1.0 + gate_part * (1.0 - sigmoid_gate))
        ).astype(low)
        up_out[:, columns] = (hidden_grad * silu_gate).astype(low)
    for start in range(0, MODEL_WIDTH, FEEDFORWARD_COLUMNS):
        across = slice(start, start + FEEDFORWARD_COLUMNS)
        back = dot(gate_out[...], weight[across, :size], 1, 1)
        back = back + dot(up_out[...], weight[across, size : 2 * size], 1, 1)
        down = dot(hidden_out[...], weight[across, 2 * size :], 1, 1)
        if before:
            back = back + before[0][:, across].astype(wide)
            down = down + before[1][:, across].astype(wide)
        back_out[:, across] = back.astype(low)
        down_out[:, across] = down.astype(low)


def feedforward(core, rows, upstream, weights, before=()):
    count = rows.shape[0]
    hidden = weights.shape[2] // 3

    def block(columns):
        return pl.BlockSpec((FEEDFORWARD_ROWS, columns), lambda index, core: (index, 0))

    return pl.pallas_call(
        feedforward_kernel,
        grid_spec=pltpu.PrefetchScalarGridSpec(
            num_scalar_prefetch=1,
            grid=(count // FEEDFORWARD_ROWS,),
            in_specs=[
                block(MODEL_WIDTH),
                block(MODEL_WIDTH),
                pl.BlockSpec(
                    (1, *weights.shape[1:]),
                    lambda index, core: (core[0], 0, 0),
                    pipeline_mode=pl.Buffered(1),
                ),
            ]
            + [block(MODEL_WIDTH)] * len(before),
            out_specs=[block(hidden)] * 3 + [block(MODEL_WIDTH)] * 2,
        ),
        out_shape=[jax.ShapeDtypeStruct((count, hidden), low)] * 3
        + [jax.ShapeDtypeStruct((count, MODEL_WIDTH), low)] * 2,
        compiler_params=pltpu.CompilerParams(vmem_limit_bytes=52 * 2**20),
        cost_estimate=pl.CostEstimate(
            flops=12 * count * MODEL_WIDTH * hidden,
            bytes_accessed=48 * 2**20,
            transcendentals=count * hidden,
        ),
        name="feedforward_more" if before else "feedforward",
    )(core, rows, upstream, weights, *before)


def head_rows(values, gain, cosine, sine):
    factor = lax.rsqrt(jnp.mean(values * values, axis=-1, keepdims=True) + norm_epsilon)
    normed = values * factor * gain
    return (normed * cosine + pltpu.roll(normed, HEAD_WIDTH // 2, 1) * sine).astype(low)


def head_back(values, gain, cosine, sine, upstream):
    turned = upstream * cosine - pltpu.roll(upstream, HEAD_WIDTH // 2, 1) * sine
    return norm_back_rows(values, gain, turned)


def head_at(index):
    return slice(index * HEAD_WIDTH, (index + 1) * HEAD_WIDTH)


def gate_column(logits, head):
    lanes = lax.broadcasted_iota(jnp.int32, logits.shape, 1)
    logit = jnp.sum(jnp.where(lanes == head, logits, 0.0), axis=-1, keepdims=True)
    return jax.nn.sigmoid(logit)


def probabilities(queries, keys, start, valid_count, piece_start):
    raw = dot(queries, keys, 1, 1) * HEAD_WIDTH ** (-0.5)
    row = start + lax.broadcasted_iota(jnp.int32, raw.shape, 0)
    column = lax.broadcasted_iota(jnp.int32, raw.shape, 1)
    last = piece_start + PIC
    inside = (row >= piece_start) & (row < last) & (column >= piece_start) & (column < last)
    allowed = (column < valid_count) & ((column <= row) | inside)
    scores = jnp.where(allowed, raw, masked_score)
    expos = jnp.exp(scores - jnp.max(scores, axis=-1, keepdims=True))
    return expos * (1.0 / jnp.sum(expos, axis=-1, keepdims=True))


QUERY_ROWS = 256


def attention_forward_kernel(groups, share, valid, start, pre, gains, cosine, sine, gated):
    sequence = pl.program_id(0)
    heads = groups * share
    length = pre.shape[0]
    for group in range(groups):
        keys = head_rows(pre[:, head_at(heads + group)], gains[1:2, :], cosine[...], sine[...])
        values = pre[:, head_at(heads + groups + group)].astype(low)
        for head in range(group * share, (group + 1) * share):
            for at in range(0, length, QUERY_ROWS):
                rows = slice(at, at + QUERY_ROWS)
                queries = head_rows(
                    pre[rows, head_at(head)], gains[0:1, :], cosine[rows, :], sine[rows, :]
                )
                probs = probabilities(queries, keys, at, valid[sequence], start[sequence])
                mixed = dot(probs.astype(low), values, 1, 0)
                gate = gate_column(pre[rows, head_at(heads + 2 * groups)], head)
                gated[rows, head_at(head)] = (mixed * gate).astype(low)


def attention_backward_kernel(
    groups, share, valid, start, pre, upstream, gains, cosine, sine, grads, gain_grads
):
    sequence = pl.program_id(0)
    heads = groups * share
    length = pre.shape[0]
    scale = HEAD_WIDTH ** (-0.5)

    @pl.when(sequence == 0)
    def _():
        gain_grads[...] = jnp.zeros_like(gain_grads)

    logit_grads = [jnp.zeros((QUERY_ROWS, HEAD_WIDTH), wide)] * (length // QUERY_ROWS)
    for group in range(groups):
        key_pre = pre[:, head_at(heads + group)]
        keys = head_rows(key_pre, gains[1:2, :], cosine[...], sine[...])
        values = pre[:, head_at(heads + groups + group)].astype(low)
        value_grad = jnp.zeros((length, HEAD_WIDTH), wide)
        key_grad = jnp.zeros((length, HEAD_WIDTH), wide)
        for head in range(group * share, (group + 1) * share):
            for block, at in enumerate(range(0, length, QUERY_ROWS)):
                rows = slice(at, at + QUERY_ROWS)
                query_pre = pre[rows, head_at(head)]
                queries = head_rows(query_pre, gains[0:1, :], cosine[rows, :], sine[rows, :])
                probs = probabilities(queries, keys, at, valid[sequence], start[sequence])
                probs_low = probs.astype(low)
                mixed = dot(probs_low, values, 1, 0)
                gate = gate_column(pre[rows, head_at(heads + 2 * groups)], head)
                gated_grad = upstream[rows, head_at(head)]
                mixed_grad = (gated_grad * gate).astype(low)
                logit_grad = (
                    jnp.sum(gated_grad * mixed, axis=-1, keepdims=True) * gate * (1.0 - gate)
                )
                lanes = lax.broadcasted_iota(jnp.int32, (QUERY_ROWS, HEAD_WIDTH), 1)
                logit_grads[block] = logit_grads[block] + jnp.where(lanes == head, logit_grad, 0.0)
                value_grad = value_grad + dot(probs_low, mixed_grad, 0, 0)
                prob_grad = dot(mixed_grad, values, 1, 1)
                score_grad = (
                    probs * (prob_grad - jnp.sum(prob_grad * probs, axis=-1, keepdims=True))
                ).astype(low)
                key_grad = key_grad + dot(score_grad, queries, 0, 0)
                query_grad, gained = head_back(
                    query_pre,
                    gains[0:1, :],
                    cosine[rows, :],
                    sine[rows, :],
                    dot(score_grad, keys, 1, 0) * scale,
                )
                grads[rows, head_at(head)] = query_grad.astype(low)
                gain_grads[0:1, :] += gained
        key_grad, gained = head_back(
            key_pre, gains[1:2, :], cosine[...], sine[...], key_grad * scale
        )
        gain_grads[1:2, :] += gained
        grads[:, head_at(heads + group)] = key_grad.astype(low)
        grads[:, head_at(heads + groups + group)] = value_grad.astype(low)
    for block, at in enumerate(range(0, length, QUERY_ROWS)):
        grads[slice(at, at + QUERY_ROWS), head_at(heads + 2 * groups)] = logit_grads[block].astype(
            low
        )


def sequence_block(columns, length):
    return pl.BlockSpec((length, columns), lambda sequence: (sequence, 0))


def fixed_block(*shape):
    return pl.BlockSpec(shape, lambda sequence: (0, 0))


SCALARS = pl.BlockSpec(memory_space=pltpu.SMEM)


def attention_forward(groups, share, valid, start, pre, gains, cosine, sine):
    length, columns = cosine.shape[0], groups * share * HEAD_WIDTH

    def body(*refs):
        attention_forward_kernel(groups, share, *refs)

    return pl.pallas_call(
        body,
        grid=(pre.shape[0] // length,),
        out_shape=jax.ShapeDtypeStruct((pre.shape[0], columns), low),
        in_specs=[
            SCALARS,
            SCALARS,
            sequence_block(pre.shape[1], length),
            fixed_block(2, HEAD_WIDTH),
            fixed_block(length, HEAD_WIDTH),
            fixed_block(length, HEAD_WIDTH),
        ],
        out_specs=sequence_block(columns, length),
        compiler_params=pltpu.CompilerParams(vmem_limit_bytes=48 * 2**20),
        cost_estimate=pl.CostEstimate(
            flops=2**30, bytes_accessed=8 * 2**20, transcendentals=2**21
        ),
        name="attention_forward",
    )(valid, start, pre, gains, cosine, sine)


def attention_backward(groups, share, valid, start, pre, upstream, gains, cosine, sine):
    length = cosine.shape[0]

    def body(*refs):
        attention_backward_kernel(groups, share, *refs)

    return pl.pallas_call(
        body,
        grid=(pre.shape[0] // length,),
        out_shape=[
            jax.ShapeDtypeStruct(pre.shape, low),
            jax.ShapeDtypeStruct((2, HEAD_WIDTH), wide),
        ],
        in_specs=[
            SCALARS,
            SCALARS,
            sequence_block(pre.shape[1], length),
            sequence_block(upstream.shape[1], length),
            fixed_block(2, HEAD_WIDTH),
            fixed_block(length, HEAD_WIDTH),
            fixed_block(length, HEAD_WIDTH),
        ],
        out_specs=[sequence_block(pre.shape[1], length), fixed_block(2, HEAD_WIDTH)],
        compiler_params=pltpu.CompilerParams(vmem_limit_bytes=48 * 2**20),
        cost_estimate=pl.CostEstimate(
            flops=2**32, bytes_accessed=12 * 2**20, transcendentals=2**21
        ),
        name="attention_backward",
    )(valid, start, pre, upstream, gains, cosine, sine)


def adam_kernel(layouts, names, heads, *refs):
    sources, refs = dict(zip(names, refs)), refs[len(names) :]
    count = len(layouts)
    stats, inverse, refs = refs[0], refs[1], refs[2:]
    small, refs = refs[:9], refs[9:]
    states, refs = refs[: 3 * count], refs[3 * count :]
    scales, small_targets, refs = refs[0], refs[1:10], refs[10:]
    targets, refs = refs[: 3 * count], refs[3 * count :]
    buffers, semaphores = refs[: 3 * count], refs[3 * count]
    loads = [
        pltpu.make_async_copy(states[i], buffers[i], semaphores.at[0, i]) for i in range(3 * count)
    ]
    stores = [
        pltpu.make_async_copy(buffers[i], targets[i], semaphores.at[1, i])
        for i in range(3 * count)
    ]
    for load in loads:
        load.start()

    def update(part, at, gradient, rate, decay_rate):
        old = (small[3 * part + i][at] for i in range(3))
        for i, value in enumerate(adam_update(*old, gradient, rate, decay_rate)):
            small_targets[3 * part + i][at] = value

    everything = (slice(None), slice(None))
    update(0, everything, stats[0:2, :], 0.5, 0.0)
    for row in range(2):
        update(1, (slice(row, row + 1), slice(None)), stats[2:3, head_at(row)], 0.5, 0.0)
    column, size = heads
    projected = sources["projected"]
    gradient = jnp.concatenate(
        [projected[core, :, column : column + 128][:, :size].astype(wide) for core in range(2)],
        axis=1,
    )
    update(2, everything, gradient, layouts[0][1], weight_decay)
    lanes = lax.broadcasted_iota(jnp.int32, scales.shape, 1)
    squares = stats[2:3, head_at(2)]
    squares = jnp.where(lanes == 2, jnp.sum(stats[3:4, :], axis=-1, keepdims=True), squares)
    scales[...] = jnp.sqrt(squares * inverse[...])
    for number, (transposed, rate, leads) in enumerate(layouts):
        matrix = buffers[3 * number : 3 * number + 3]
        for load in loads[3 * number : 3 * number + 3]:
            load.wait()
        for lead, pieces in enumerate(leads):
            quarter = sum(size for _, _, size in pieces)
            for core in range(2):
                start = core * quarter
                for name, column, size in pieces:
                    step = 256 if size % 256 == 0 else 128

                    @pl.loop(0, size // step)
                    def _(block):
                        columns = pl.ds(pl.multiple_of(column + block * step, 128), step)
                        gradient = sources[name][core, :, columns].astype(wide)
                        place = pl.ds(pl.multiple_of(start + block * step, 128), step)
                        if transposed:
                            gradient = gradient.T
                            at = (place, slice(None))
                        elif len(leads) > 1:
                            at = (lead, slice(None), place)
                        else:
                            at = (slice(None), place)
                        weight, moment, square = (part[at] for part in matrix)
                        for part, value in zip(
                            matrix,
                            adam_update(weight, moment, square, gradient, rate, weight_decay),
                        ):
                            part[at] = value

                    start += size
        for store in stores[3 * number : 3 * number + 3]:
            store.start()
    for store in stores:
        store.wait()


def adam_matrices(layouts, heads, sums, stats, inverse, small, states):
    def body(*refs):
        adam_kernel(layouts, list(sums), heads, *refs)

    def like(values):
        return [jax.ShapeDtypeStruct(value.shape, value.dtype) for value in values]

    return pl.pallas_call(
        body,
        out_shape=like([inverse, *small, *states]),
        in_specs=[VMEM] * (len(sums) + 2 + len(small)) + [ANY] * len(states),
        out_specs=[VMEM] * (1 + len(small)) + [ANY] * len(states),
        scratch_shapes=[pltpu.VMEM(value.shape, value.dtype) for value in states]
        + [pltpu.SemaphoreType.DMA((2, len(states)))],
        compiler_params=pltpu.CompilerParams(vmem_limit_bytes=48 * 2**20),
        cost_estimate=pl.CostEstimate(
            flops=2**25, bytes_accessed=40 * 2**20, transcendentals=2**21
        ),
        name="adam_matrices",
    )(*sums.values(), stats, inverse, *small, *states)


def local(
    tokens,
    cotangent,
    valid_len,
    pic_start,
    norm_gains,
    norm_moment,
    norm_square,
    head_gains,
    head_moment,
    head_square,
    query_weight,
    query_moment,
    query_square,
    keyvalue_matrix,
    keyvalue_first_moment,
    keyvalue_second_moment,
    headgate_weight,
    headgate_moment,
    headgate_square,
    output_weight,
    output_moment,
    output_square,
    gateup_weight,
    gateup_moment,
    gateup_square,
    down_weight,
    down_moment,
    down_square,
):
    local_rows = tokens.shape[0]
    length_value = local_rows * 2
    rows = length_value * 2
    group = lax.axis_index("w")
    core = lax.axis_index("c")
    place = lax.axis_index("t")
    heads_here = query_weight.shape[1] // HEAD_WIDTH // 2
    groups_here = keyvalue_matrix.shape[2] // HEAD_WIDTH // 2
    share = heads_here // groups_here
    head_cols = heads_here * HEAD_WIDTH
    group_cols = groups_here * HEAD_WIDTH
    hidden_here = gateup_weight.shape[2] // 2

    bounds = [0, head_cols, group_cols, group_cols, 128, head_cols]
    edges = [sum(bounds[: i + 1]) for i in range(6)]
    quarters = []
    for index in range(2):
        pieces = []
        for matrix in (
            query_weight, keyvalue_matrix[0], keyvalue_matrix[1], headgate_weight, output_weight.T
        ):
            size = matrix.shape[1] // 2
            piece = matrix[:, index * size : (index + 1) * size].astype(low)
            pieces.append(jnp.pad(piece, ((0, 0), (0, -size % 128))))
        quarters.append(jnp.concatenate(pieces, axis=1))
    matrices = (gateup_weight[0], gateup_weight[1], down_weight.T)
    sizes = (hidden_here - hidden_here // 6, hidden_here // 6)

    def quarter_columns(index, start, size):
        return jnp.concatenate(
            [
                matrix[:, index * hidden_here + start : index * hidden_here + start + size].astype(
                    low
                )
                for matrix in matrices
            ],
            axis=1,
        )

    large_block, small_block = (
        jnp.stack([quarter_columns(index, start, size) for index in range(2)])
        for start, size in zip((0, sizes[0]), sizes)
    )
    residual = tokens.astype(wide)
    mine, other, normed, large_block, small_block = lax.optimization_barrier(
        (
            jnp.where(core == 0, quarters[0], quarters[1]),
            jnp.where(core == 0, quarters[1], quarters[0]),
            normalize(residual, norm_gains[0]).astype(low),
            large_block,
            small_block,
        )
    )
    large_both = lax.all_gather(large_block, ("w", "c"), axis=1, tiled=True)
    small_both = lax.all_gather(small_block, ("w", "c"), axis=1, tiled=True)
    attention_full, first_full, output_grad_full = gather_attention(mine, other, normed, cotangent)
    projection_full, output_full = attention_full[:, : edges[4]], attention_full[:, edges[4] :]
    valid_pair = lax.dynamic_slice_in_dim(valid_len, 2 * group, 2)
    start_pair = lax.dynamic_slice_in_dim(pic_start, 2 * group, 2)
    cosine, sine = rotary_tables(length_value)
    projected = dot(first_full, projection_full, 1, 0)
    gated_low = attention_forward(
        groups_here, share, valid_pair, start_pair, projected, head_gains, cosine, sine
    )
    attention_local, second_full = exchange_forward(
        dot(gated_low, output_full, 1, 1).astype(low), tokens, norm_gains[1:2]
    )
    middle = residual + attention_local
    gate_large, up_large, hidden_large, *before = feedforward(
        core[None], second_full, output_grad_full, large_both
    )
    gate_small, up_small, hidden_small, second_partial, feedforward_partial = feedforward(
        core[None], second_full, output_grad_full, small_both, before
    )
    own_places = place * local_rows + jnp.arange(local_rows, dtype=jnp.int32)
    counted = (own_places < valid_pair[core]).astype(wide)[:, None]
    half = sizes[0] // 2
    pieces = [(0, half), (half, sizes[0] - half)]
    middle_grad, second_gain_grad, feedforward_local, output_squares, attention_grad, *sums = (
        exchange_backward(
            second_partial,
            feedforward_partial,
            middle,
            cotangent,
            norm_gains[1:2],
            counted,
            [
                (second_full, grad, *piece) for grad in (gate_large, up_large) for piece in pieces
            ]
            + [(second_full, grad, 0, sizes[1]) for grad in (gate_small, up_small)],
        )
    )
    block_output = (middle + feedforward_local).astype(low)
    projected_grad, head_gain_grads = attention_backward(
        groups_here,
        share,
        valid_pair,
        start_pair,
        projected,
        dot(attention_grad, output_full, 1, 0),
        head_gains,
        cosine,
        sine,
    )
    first_partial = dot(projected_grad, projection_full, 1, 1)
    squares = jnp.stack(
        [
            jnp.sum(counted * residual * residual),
            jnp.sum(counted * attention_local * attention_local),
        ]
    )
    small = jnp.concatenate([head_gain_grads.reshape(-1), squares])
    nothing = jnp.zeros((1, MODEL_WIDTH), wide)
    stats = jnp.concatenate(
        [
            nothing,
            second_gain_grad,
            jnp.pad(small, (0, MODEL_WIDTH - small.shape[0]))[None],
            output_squares,
            jnp.tile(nothing, (4, 1)),
        ]
    )
    tokens_grad, stats, projected_sums, output_sums, *more = exchange_last(
        first_partial.astype(low),
        tokens,
        norm_gains[0:1],
        middle_grad,
        stats,
        [
            (first_full, projected_grad, 0, edges[4]),
            (attention_grad, gated_low, 0, head_cols),
        ]
        + [(output_grad_full, hidden_large, *piece) for piece in pieces]
        + [(output_grad_full, hidden_small, 0, sizes[1])],
    )
    denominator = jnp.sum(valid_len).astype(wide) * MODEL_WIDTH
    inverse = jnp.full((1, HEAD_WIDTH), 1.0 / denominator)
    input_rate = MODEL_WIDTH ** (-0.5)
    down_rate = FF ** (-0.5)
    output_rate = max(QUERY_HEADS * HEAD_WIDTH // 128, 4) ** (-0.5)
    widths = [half, sizes[0] - half, sizes[1]]

    def parts_of(name):
        return [(f"{name} {index}", 0, width) for index, width in enumerate(widths)]

    layouts = [
        (
            False,
            input_rate,
            [parts_of("gate"), parts_of("up")],
        ),
        (True, down_rate, [parts_of("down")]),
        (False, input_rate, [[("projected", edges[0], head_cols)]]),
        (
            False,
            input_rate,
            [[("projected", edges[1], group_cols)], [("projected", edges[2], group_cols)]],
        ),
        (True, output_rate, [[("output", 0, head_cols)]]),
    ]
    names = ["gate 0", "gate 1", "up 0", "up 1", "gate 2", "up 2", "down 0", "down 1", "down 2"]
    sums = dict(zip(names, [*sums, *more]))
    sums["projected"], sums["output"] = projected_sums, output_sums
    scales, *updated = adam_matrices(
        layouts,
        (edges[3], heads_here),
        sums,
        stats,
        inverse,
        [
            norm_gains,
            norm_moment,
            norm_square,
            head_gains,
            head_moment,
            head_square,
            headgate_weight,
            headgate_moment,
            headgate_square,
        ],
        [
            gateup_weight,
            gateup_moment,
            gateup_square,
            down_weight,
            down_moment,
            down_square,
            query_weight,
            query_moment,
            query_square,
            keyvalue_matrix,
            keyvalue_first_moment,
            keyvalue_second_moment,
            output_weight,
            output_moment,
            output_square,
        ],
    )
    norms_new, heads_new, headgate_new, gateup_new, down_new, query_new, keyvalue_new, output_new = (
        updated[3 * i : 3 * i + 3] for i in range(8)
    )
    branch_scales = scales[0, :3]
    return (
        block_output,
        tokens_grad,
        branch_scales,
        *norms_new,
        *heads_new,
        *query_new,
        *keyvalue_new,
        *headgate_new,
        *output_new,
        *gateup_new,
        *down_new,
    )


def solution(mesh):
    fsdp, tp = mesh.devices.shape
    fine = Mesh(mesh.devices.reshape(fsdp // 2, 2, tp), ("w", "c", "t"))
    whole = ("w", "c")
    rows = P(("w", "c", "t"), None)
    first = P(whole, "t")
    second = P(None, whole, "t")
    last = P("t", whole)
    matrices = (first,) * 3 + (second,) * 3 + (first,) * 3 + (last,) * 3 + (second,) * 3 + (last,) * 3
    return jax.shard_map(
        local,
        mesh=fine,
        in_specs=(rows, rows, P(), P()) + (P(),) * 6 + matrices,
        out_specs=(rows, rows, P()) + (P(),) * 6 + matrices,
        check_vma=False,
    )
```

profile of v0, /device:TPU:0, one launch (start us, length us, event | category | flops | bytes accessed | tf_op | source)
XLA Modules:
  0.0 710.0 jit_solution(10649105893372889936)
XLA Ops:
  7.3 2.1 fusion.15
  9.4 0.9 fusion.26
  12.1 0.9 fusion.28
  17.4 1.3 dynamic_slice.14
  19.5 1.3 fusion.11
  21.4 1.3 fusion.10.first
  23.0 1.4 pad_maximum_fusion
  25.5 1.0 broadcast_select_fusion
  29.6 149.8 %gather_attention.1 = (bf16[2048,1664]{1,0:T(8,128)(2,1)}, bf16[1024,2048]{1,0:T(8,128)(2,1)}, bf16[1024,2048]{1,0:T(8,128)(2,1)}) custom-call(bf16[128,1664]{1,0:T(8,128)(2,1)} %get-tuple-element.92.mine, bf16[128,1664]{1,0:T(8,128)(2,1)} %get-tuple-element.93.other, bf16[256,2048]{1,0:T(8,128)(2,1)} %fusion.10.first, bf16[256,2048]{1,0:T(8,128)(2,1)} %refs_3_.3), custom_call_target="tpu_custom_call" | custom-call | bytes 67108864 | tf_op jit(solution)/shard_map/gather_attention/pallas_call | solution.py:503
  179.4 1.0 fusion.22
  180.7 10.6 %fusion.2.refs_2_ = f32[1024,1152]{1,0:T(8,128)} fusion(bf16[1024,2048]{1,0:T(8,128)(2,1)} %get-tuple-element.95.refs_5_, bf16[2048,1664]{1,0:T(8,128)(2,1)} %get-tuple-element.96), kind=kOutput, calls=%fused_computation.7 | convolution fusion | flops 4831838208 | bytes 13631488 | tf_op jit(solution)/shard_map/dot_general | solution.py:64
  191.3 12.0 %attention_forward.1.refs_8_ = bf16[1024,512]{1,0:T(8,128)(2,1)S(1)} custom-call(s32[2]{0:T(128)S(1)} %dynamic_slice.11.refs_0_, s32[2]{0:T(128)S(1)} %dynamic_slice.12.refs_1_, f32[1024,1152]{1,0:T(8,128)} %fusion.2.refs_2_, f32[2,128]{1,0:T(2,128)S(1)} %copy-done.29, f32[512,128]{1,0:T(8,128)S(1)} %get-tuple-element.254.refs_4_.refs_5_, ...), custom_call_target="tpu_custom_call" | custom-call | flops 1073741824 | bytes 8388608 | tf_op jit(solution)/shard_map/attention_forward/pallas_call | solution.py:995
  203.3 6.4 convolution_convert_fusion.partial
  209.6 55.1 %exchange_forward.1 = (f32[256,2048]{1,0:T(8,128)}, bf16[1024,2048]{1,0:T(8,128)(2,1)}) custom-call(bf16[1024,2048]{1,0:T(8,128)(2,1)} %convolution_convert_fusion.partial, bf16[256,2048]{1,0:T(8,128)(2,1)} %refs_1_.1, f32[1,2048]{1,0:T(1,128)} %get-tuple-element.243.gain.refs_4_), custom_call_target="tpu_custom_call" | custom-call | bytes 67108864 | tf_op jit(solution)/shard_map/exchange_forward/pallas_call | solution.py:546
  264.8 1.3 fusion.21.refs_5_
  266.1 3.8 fusion.7
  269.9 43.3 %feedforward.1 = (bf16[1024,1280]{1,0:T(8,128)(2,1)}, bf16[1024,1280]{1,0:T(8,128)(2,1)}, bf16[1024,1280]{1,0:T(8,128)(2,1)}, bf16[1024,2048]{1,0:T(8,128)(2,1)}, bf16[1024,2048]{1,0:T(8,128)(2,1)}) custom-call(s32[1]{0:T(128)} %bitcast.11.core, bf16[1024,2048]{1,0:T(8,128)(2,1)} %get-tuple-element.98.rows.refs_6_, ...), custom_call_target="tpu_custom_call" | custom-call | flops 32212254720 | bytes 50331648 | tf_op jit(solution)/shard_map/feedforward/pallas_call | solution.py:832
  313.2 3.0 all-gather.3.cloned.1.call-done.weights
  316.2 15.1 %feedforward_more.1 = (bf16[1024,256]{1,0:T(8,128)(2,1)S(1)}, bf16[1024,256]{1,0:T(8,128)(2,1)S(1)}, bf16[1024,256]{1,0:T(8,128)(2,1)S(1)}, bf16[1024,2048]{1,0:T(8,128)(2,1)}, bf16[1024,2048]{1,0:T(8,128)(2,1)}) custom-call(s32[1]{0:T(128)} %bitcast.11.core, bf16[1024,2048]{1,0:T(8,128)(2,1)} %get-tuple-element.98.rows.refs_6_, ...), custom_call_target="tpu_custom_call" | custom-call | flops 6442450944 | bytes 50331648 | tf_op jit(solution)/shard_map/feedforward_more/pallas_call | solution.py:832
  333.7 155.1 %exchange_backward.1 = (f32[256,2048]{1,0:T(8,128)}, f32[1,2048]{1,0:T(1,128)}, f32[256,2048]{1,0:T(8,128)}, f32[1,2048]{1,0:T(1,128)}, bf16[1024,2048]{1,0:T(8,...) custom-call(bf16[1024,2048]{1,0:T(8,128)(2,1)} %get-tuple-element.10, ...), custom_call_target="tpu_custom_call" | custom-call | bytes 134217728 | tf_op jit(solution)/shard_map/exchange_backward/pallas_call | solution.py:650
  488.9 5.3 fusion.12.refs_3_
  494.3 23.5 %attention_backward.1 = (bf16[1024,1152]{1,0:T(8,128)(2,1)S(1)}, f32[2,128]{1,0:T(2,128)S(1)}) custom-call(s32[2]{0:T(128)S(1)} %copy-done.35, s32[2]{0:T(128)S(1)} %copy-done.37, f32[1024,1152]{1,0:T(8,128)} %fusion.2.refs_2_, f32[1024,512]{1,0:T(8,128)S(1)} %fusion.12.refs_3_, f32[2,128]{1,0:T(2,128)S(1)} %copy-done.30, f32[512,128]{1,0:T(8,128)S(1)} %copy-done.5, ...), custom_call_target="tpu_custom_call" | custom-call | flops 4294967296 | bytes 12582912 | tf_op jit(solution)/shard_map/attention_backward/pallas_call | solution.py:1022
  517.9 7.4 %fusion.4.refs_0_ = bf16[1024,2048]{1,0:T(8,128)(2,1)} fusion(bf16[1024,1152]{1,0:T(8,128)(2,1)S(1)} %get-tuple-element.112.refs_6_, bf16[2048,1664]{1,0:T(8,128)(2,1)S(1)} %bitcast.42), kind=kOutput, calls=%fused_computation.9 | convolution fusion | flops 4833935360 | bytes 11272192 | tf_op jit(solution)/shard_map/dot_general | solution.py:64
  525.3 1.4 select_maximum_fusion
  527.5 148.2 %exchange_last.1 = (f32[256,2048]{1,0:T(8,128)}, f32[8,2048]{1,0:T(8,128)}, bf16[2,128,1152]{2,1,0:T(8,128)(2,1)}, bf16[2,128,512]{2,1,0:T(8,128)(2,1)}, bf16[2,...) custom-call(bf16[1024,2048]{1,0:T(8,128)(2,1)} %fusion.4.refs_0_, ...), custom_call_target="tpu_custom_call" | custom-call | bytes 134217728 | tf_op jit(solution)/shard_map/exchange_last/pallas_call | solution.py:766
  676.0 1.0 copy-done.18
  676.9 1.0 copy-done.19
  677.9 0.9 copy-done.20
  678.9 0.9 copy-done.24
  680.6 15.6 %adam_matrices.1 = (f32[1,128]{1,0:T(1,128)S(1)}, f32[2,2048]{1,0:T(2,128)}, f32[2,2048]{1,0:T(2,128)}, f32[2,2048]{1,0:T(2,128)}, f32[2,128]{1,0:T(2,128)}, /*i...) custom-call(bf16[2,128,640]{2,1,0:T(8,128)(2,1)S(1)} %copy-done.14, ...), custom_call_target="tpu_custom_call" | custom-call | flops 33554432 | bytes 41943040 | tf_op jit(solution)/shard_map/adam_matrices/pallas_call | solution.py:1130
  698.7 2.9 add_convert_fusion
  701.6 1.3 copy.83
  (183 shorter events, 18.0 us)
Async XLA Ops:
  7.2 262.7 %all-gather.5.cloned.1.call-start = ((), (), s32[]{:S(2)}) async-start(), calls=%async_computation.1 | async-start | bytes 33423360 | tf_op jit(solution)/shard_map/all_gather | solution.py:1228
  13.0 7.8 %copy-start.26 = (f32[2,2048]{1,0:T(2,128)S(1)}, f32[2,2048]{1,0:T(2,128)}, u32[]{:S(2)}) copy-start(f32[2,2048]{1,0:T(2,128)} %refs_13_.1) | copy-start | bytes 49156
  14.4 8.3 %copy-start.44 = (bf16[128,1280]{1,0:T(8,128)(2,1)S(1)}, bf16[128,1280]{1,0:T(8,128)(2,1)}, u32[]{:S(2)}) copy-start(bf16[128,1280]{1,0:T(8,128)(2,1)} %get-tuple-element.225) | copy-start | bytes 983044
  14.4 8.3 %copy-start.45 = (bf16[128,1280]{1,0:T(8,128)(2,1)S(1)}, bf16[128,1280]{1,0:T(8,128)(2,1)}, u32[]{:S(2)}) copy-start(bf16[128,1280]{1,0:T(8,128)(2,1)} %get-tuple-element.226) | copy-start | bytes 983044
  26.5 289.7 %all-gather.3.cloned.1.call-start = ((), (), s32[]{:S(2)}) async-start(), calls=%async_computation | async-start | bytes 6684672 | tf_op jit(solution)/shard_map/all_gather | solution.py:1229
  27.4 163.9 %copy-start.34 = (s32[2]{0:T(128)}, s32[2]{0:T(128)S(1)}, u32[]{:S(2)}) copy-start(s32[2]{0:T(128)S(1)} %dynamic_slice.11.refs_0_) | copy-start | bytes 28
  28.1 163.2 %copy-start.36 = (s32[2]{0:T(128)}, s32[2]{0:T(128)S(1)}, u32[]{:S(2)}) copy-start(s32[2]{0:T(128)S(1)} %dynamic_slice.12.refs_1_) | copy-start | bytes 28
  180.6 10.6 %copy-start.4 = (f32[512,128]{1,0:T(8,128)}, f32[512,128]{1,0:T(8,128)S(1)}, u32[]{:S(2)}) copy-start(f32[512,128]{1,0:T(8,128)S(1)} %get-tuple-element.254.refs_4_.refs_5_) | copy-start | bytes 786436
  180.6 10.6 %copy-start.6 = (f32[512,128]{1,0:T(8,128)}, f32[512,128]{1,0:T(8,128)S(1)}, u32[]{:S(2)}) copy-start(f32[512,128]{1,0:T(8,128)S(1)} %get-tuple-element.255.refs_5_.refs_6_) | copy-start | bytes 786436
  180.7 10.6 %copy-start.29 = (f32[2,128]{1,0:T(2,128)S(1)}, f32[2,128]{1,0:T(2,128)}, u32[]{:S(2)}) copy-start(f32[2,128]{1,0:T(2,128)} %refs_16_.1) | copy-start | bytes 3076
  209.6 56.5 %copy-start.39 = (bf16[256,2048]{1,0:T(8,128)(2,1)S(1)}, bf16[256,2048]{1,0:T(8,128)(2,1)}, u32[]{:S(2)}) copy-start(bf16[256,2048]{1,0:T(8,128)(2,1)} %refs_1_.1) | copy-start | bytes 3145732
  209.6 56.5 %copy-start.63 = (f32[256]{0:T(256)S(1)}, f32[256]{0:T(256)}, u32[]{:S(2)}) copy-start(f32[256]{0:T(256)} %copy-done.62) | copy-start | bytes 3076
  333.7 184.1 %slice-start = ((s8[6815744]{0:T(1024)(128)(4,1)}), s8[2621440]{0:T(1024)(128)(4,1)S(1)}, s32[]{:S(2)}) async-start(s8[6815744]{0:T(1024)(128)(4,1)} %bitcast.41), calls=%async_computation.2 | async-start | bytes 5242880
  488.9 29.0 %slice-start.1 = ((s8[6815744]{0:T(1024)(128)(4,1)}), s8[4194304]{0:T(1024)(128)(4,1)S(1)}, s32[]{:S(2)}) async-start(s8[6815744]{0:T(1024)(128)(4,1)} %bitcast.41), calls=%async_computation.3 | async-start | bytes 8388608
  517.9 8.8 %copy-start.64 = (f32[1,2048]{1,0:T(1,128)S(1)}, f32[1,2048]{1,0:T(1,128)}, u32[]{:S(2)}) copy-start(f32[1,2048]{1,0:T(1,128)} %get-tuple-element.114) | copy-start | bytes 24580
  517.9 8.8 %copy-start.65 = (f32[1,2048]{1,0:T(1,128)S(1)}, f32[1,2048]{1,0:T(1,128)}, u32[]{:S(2)}) copy-start(f32[1,2048]{1,0:T(1,128)} %get-tuple-element.116) | copy-start | bytes 24580
  527.4 148.4 %copy-start.8 = (f32[128,1024]{1,0:T(8,128)S(1)}, f32[128,1024]{1,0:T(8,128)}, u32[]{:S(2)}) copy-start(f32[128,1024]{1,0:T(8,128)} %refs_29_.1) | copy-start | bytes 1572868
  527.4 148.4 %copy-start.9 = (f32[128,1024]{1,0:T(8,128)S(1)}, f32[128,1024]{1,0:T(8,128)}, u32[]{:S(2)}) copy-start(f32[128,1024]{1,0:T(8,128)} %refs_30_.1) | copy-start | bytes 1572868
  527.4 148.4 %copy-start.10 = (f32[2,128,512]{2,1,0:T(8,128)S(1)}, f32[2,128,512]{2,1,0:T(8,128)}, u32[]{:S(2)}) copy-start(f32[2,128,512]{2,1,0:T(8,128)} %refs_32_.1) | copy-start | bytes 1572868
  527.4 148.4 %copy-start.14 = (bf16[2,128,640]{2,1,0:T(8,128)(2,1)S(1)}, bf16[2,128,640]{2,1,0:T(8,128)(2,1)}, u32[]{:S(2)}) copy-start(bf16[2,128,640]{2,1,0:T(8,128)(2,1)} %get-tuple-element.120.refs_0_) | copy-start | bytes 983044
  527.4 148.4 %copy-start.15 = (bf16[2,128,640]{2,1,0:T(8,128)(2,1)S(1)}, bf16[2,128,640]{2,1,0:T(8,128)(2,1)}, u32[]{:S(2)}) copy-start(bf16[2,128,640]{2,1,0:T(8,128)(2,1)} %get-tuple-element.121.refs_1_) | copy-start | bytes 983044
  527.4 148.4 %copy-start.16 = (bf16[2,128,640]{2,1,0:T(8,128)(2,1)S(1)}, bf16[2,128,640]{2,1,0:T(8,128)(2,1)}, u32[]{:S(2)}) copy-start(bf16[2,128,640]{2,1,0:T(8,128)(2,1)} %get-tuple-element.122.refs_2_) | copy-start | bytes 983044
  527.4 148.4 %copy-start.17 = (bf16[2,128,640]{2,1,0:T(8,128)(2,1)S(1)}, bf16[2,128,640]{2,1,0:T(8,128)(2,1)}, u32[]{:S(2)}) copy-start(bf16[2,128,640]{2,1,0:T(8,128)(2,1)} %get-tuple-element.123.refs_3_) | copy-start | bytes 983044
  527.5 148.4 %copy-start.21 = (f32[128,8]{1,0:T(8,128)S(1)}, f32[128,8]{1,0:T(8,128)}, u32[]{:S(2)}) copy-start(f32[128,8]{1,0:T(8,128)} %copy.70.refs_21_) | copy-start | bytes 12292
  527.5 148.4 %copy-start.22 = (bf16[2,128,256]{2,1,0:T(8,128)(2,1)S(1)}, bf16[2,128,256]{2,1,0:T(8,128)(2,1)}, u32[]{:S(2)}) copy-start(bf16[2,128,256]{2,1,0:T(8,128)(2,1)} %get-tuple-element.124.refs_4_) | copy-start | bytes 393220
  527.5 148.4 %copy-start.23 = (bf16[2,128,256]{2,1,0:T(8,128)(2,1)S(1)}, bf16[2,128,256]{2,1,0:T(8,128)(2,1)}, u32[]{:S(2)}) copy-start(bf16[2,128,256]{2,1,0:T(8,128)(2,1)} %get-tuple-element.125.refs_5_) | copy-start | bytes 393220
  527.5 148.4 %copy-start.27 = (f32[2,2048]{1,0:T(2,128)S(1)}, f32[2,2048]{1,0:T(2,128)}, u32[]{:S(2)}) copy-start(f32[2,2048]{1,0:T(2,128)} %refs_14_.1) | copy-start | bytes 49156
  527.5 148.4 %copy-start.28 = (f32[2,2048]{1,0:T(2,128)S(1)}, f32[2,2048]{1,0:T(2,128)}, u32[]{:S(2)}) copy-start(f32[2,2048]{1,0:T(2,128)} %refs_15_.1) | copy-start | bytes 49156
  527.5 148.4 %copy-start.31 = (f32[2,128]{1,0:T(2,128)S(1)}, f32[2,128]{1,0:T(2,128)}, u32[]{:S(2)}) copy-start(f32[2,128]{1,0:T(2,128)} %refs_16_.1) | copy-start | bytes 3076
  527.5 148.4 %copy-start.32 = (f32[2,128]{1,0:T(2,128)S(1)}, f32[2,128]{1,0:T(2,128)}, u32[]{:S(2)}) copy-start(f32[2,128]{1,0:T(2,128)} %refs_17_.1) | copy-start | bytes 3076
  527.5 148.4 %copy-start.33 = (f32[2,128]{1,0:T(2,128)S(1)}, f32[2,128]{1,0:T(2,128)}, u32[]{:S(2)}) copy-start(f32[2,128]{1,0:T(2,128)} %refs_18_.1) | copy-start | bytes 3076
  680.6 18.1 %copy-start.40 = (f32[256,2048]{1,0:T(8,128)S(1)}, f32[256,2048]{1,0:T(8,128)}, u32[]{:S(2)}) copy-start(f32[256,2048]{1,0:T(8,128)} %get-tuple-element.216.refs_2_) | copy-start | bytes 6291460
  (42 other events, 122.1 us)
Sparse Core Ops, SparseCore 0:
  26.6 225.1 all-gather.4
  254.7 61.5 all-gather.2
where the time goes:
time: 715 us; the launch traced here: 710 us
  Pallas kernels  618 us (86%)
  matrix products  29.7 us (4%)
  local copies, waits for them, and re-layouts  24.9 us (3%)
  other arithmetic  18 us (3%)
  between operations  15.9 us (2%)
    pallas_call x1, Pallas kernels, exchange_backward(): pl.pallas_call(body, out_shape=[jax.ShapeDtypeStruct((size, MODEL_WIDTH),...  155 us
    pallas_call x1, Pallas kernels, gather_attention(): pl.pallas_call(gather_kernel, out_shape=[jax.ShapeDtypeStruct((MODEL_WIDT...  150 us
    pallas_call x1, Pallas kernels, exchange_last(): pl.pallas_call(body, out_shape=[jax.ShapeDtypeStruct((size, MODEL_WIDTH),...  148 us
    pallas_call x2, Pallas kernels, feedforward(): pl.pallas_call(feedforward_kernel, grid_spec=pltpu.PrefetchScalarGridSpec...  58.4 us
    pallas_call x1, Pallas kernels, exchange_forward(): pl.pallas_call(forward_kernel, out_shape=[jax.ShapeDtypeStruct((size, MOD...  55.1 us
    dot_general x4, matrix products, dot(): lax.dot_general(left, right, (((left_dim,), (right_dim,)), ((), ())), pre...  29.7 us
    pallas_call x1, Pallas kernels, attention_backward(): pl.pallas_call(body, grid=(pre.shape[0] // length,), out_shape=[jax.Shape...  23.5 us
    pallas_call x1, Pallas kernels, adam_matrices(): pl.pallas_call(body, out_shape=like([inverse, *small, *states]), in_specs...  15.6 us
  transfers between devices with their start and end apart: 2, of which 1 were waited for; matrix products, arithmetic and copies ran while one was open for 4% of the time, Pallas kernels for 37%

commit v1 on v0

--- a/solution.py
+++ b/solution.py
@@ -283,8 +283,9 @@
 
 
 class RingSum:
-    def __init__(self, device, grads, scratch, sums):
+    def __init__(self, device, grads, ready, scratch, sums):
         self.device, self.grads, self.sums = device, grads, sums
+        self.ready = ready
         self.slots, self.totals, self.first = scratch
         self.half = grads.rows // device.count // 2
         self.parts = grads.parts
@@ -319,6 +320,7 @@
             step, part = self.ticks.pop(0)
             starts = [self.own(way, step + 1, part) for way in range(2)]
             if step == 0:
+                self.ready()
                 sources = self.grads.sources(starts, self.part, self.first)
                 for way in range(2):
                     self.send(way, step, part, sources[way])
@@ -362,7 +364,6 @@
 
 class RingWork:
     def __init__(self, pairs):
-        self.pairs = pairs
         self.columns = [columns for _, _, _, columns in pairs]
         self.fit = (MODEL_WIDTH // lax.axis_size("w") // 2) % 128 == 0
         self.operands, self.places = [], []
@@ -380,12 +381,29 @@
         self.operands.append(value)
         return len(self.operands) - 1
 
-    def sources(self, refs):
-        sources = [
-            Product(refs[place[0]], refs[place[1]], *place[2:]) if self.fit else Given(refs[place[0]])
-            for place in self.places
-        ]
-        return sources, refs[len(self.operands) :]
+    def begin(self, device, operands, scratch, sums):
+        count = len(self.operands)
+        buffers, scratch = scratch[:count], scratch[count:]
+        loads = [device.inside(value, buffer) for value, buffer in zip(operands, buffers)]
+        for load in loads:
+            load.start()
+        waiting = set(range(count))
+        rings = []
+        for index, place in enumerate(self.places):
+            used = place[:2] if self.fit else place[:1]
+
+            def ready(used=used):
+                for number in used:
+                    if number in waiting:
+                        waiting.remove(number)
+                        loads[number].wait()
+
+            refs = [buffers[number] for number in used]
+            grads = Product(*refs, *place[2:]) if self.fit else Given(*refs)
+            rings.append(
+                RingSum(device, grads, ready, scratch[3 * index : 3 * index + 3], sums[index])
+            )
+        return Rings(rings)
 
     def outputs(self):
         half = MODEL_WIDTH // lax.axis_size("w") // 2
@@ -393,10 +411,12 @@
 
     def scratch(self):
         count = lax.axis_size("w")
-        return [shape for size in self.columns for shape in ring_shapes(size, count)]
+        return [pltpu.VMEM(value.shape, value.dtype) for value in self.operands] + [
+            shape for size in self.columns for shape in ring_shapes(size, count)
+        ]
 
     def semaphores(self):
-        return 4 * (lax.axis_size("w") + 1) * len(self.columns)
+        return 4 * (lax.axis_size("w") + 1) * len(self.columns) + len(self.operands)
 
 
 def collect_shapes(size):
@@ -589,18 +609,16 @@
 
 def backward_kernel(work, partial, output, middle, rows, gain, counted, *refs):
     count = len(work.columns)
-    grads, refs = work.sources(refs)
-    grad, gain_grad, output_total, squares, full, refs = *refs[:5], refs[5:]
+    operands, refs = refs[: len(work.operands)], refs[len(work.operands) :]
+    grad, gain_grad, block, squares, full, refs = *refs[:5], refs[5:]
     sums, refs = refs[:count], refs[count:]
     rounded = refs[8]
     device = Device(refs[-1])
+    rings = work.begin(device, operands, refs[9:-1], sums)
     device.meet(neighbours(device))
     collect = Collect(device, partial, *refs[:4])
     output_collect = Collect(device, output, *refs[4:8])
     spread = Spread(device, full)
-    rings = Rings(
-        [RingSum(device, grads[i], refs[9 + 3 * i : 12 + 3 * i], sums[i]) for i in range(count)]
-    )
     collect.start()
     rings.tick(2)
     gain_grad[...] = jnp.zeros_like(gain_grad)
@@ -618,7 +636,7 @@
         gain_grad[...] += gained
 
     def use_output(at, value):
-        output_total[at, :] = value
+        block[at, :] = (middle[at, :] + value).astype(low)
         squares[...] += jnp.sum(counted[at, :] * value * value, axis=0, keepdims=True)
 
     for index in range(BLOCKS):
@@ -652,12 +670,12 @@
         out_shape=[
             jax.ShapeDtypeStruct((size, MODEL_WIDTH), wide),
             jax.ShapeDtypeStruct((1, MODEL_WIDTH), wide),
-            jax.ShapeDtypeStruct((size, MODEL_WIDTH), wide),
+            jax.ShapeDtypeStruct((size, MODEL_WIDTH), low),
             jax.ShapeDtypeStruct((1, MODEL_WIDTH), wide),
             jax.ShapeDtypeStruct((4 * size, MODEL_WIDTH), low),
             *work.outputs(),
         ],
-        in_specs=[ANY, ANY] + [VMEM] * (4 + len(work.operands)),
+        in_specs=[ANY, ANY] + [VMEM] * 4 + [ANY] * len(work.operands),
         out_specs=[VMEM] * 4 + [ANY] * (1 + len(work.columns)),
         scratch_shapes=collect_shapes(size) * 2
         + [pltpu.VMEM((size, MODEL_WIDTH), low)]
@@ -718,19 +736,14 @@
 
 def last_kernel(work, first, tokens, gain, middle_grad, stats, *refs):
     count = len(work.columns)
-    grads, refs = work.sources(refs)
+    operands, refs = refs[: len(work.operands)], refs[len(work.operands) :]
     first_total, stats_total, refs = refs[0], refs[1], refs[2:]
     sums, scratch = refs[:count], refs[count:]
     device = Device(scratch[-1])
+    rings = work.begin(device, operands, scratch[7:-1], sums)
     device.meet(neighbours(device))
     collect = Collect(device, first, *scratch[:4])
     mine, crossed, gathered = scratch[4:7]
-    rings = Rings(
-        [
-            RingSum(device, grads[i], scratch[7 + 3 * i : 10 + 3 * i], sums[i])
-            for i in range(count)
-        ]
-    )
     total = Total(device, mine, crossed, gathered)
     mine[0] = stats[...]
     collect.start()
@@ -770,7 +783,7 @@
             jax.ShapeDtypeStruct(stats.shape, wide),
             *work.outputs(),
         ],
-        in_specs=[ANY] + [VMEM] * (4 + len(work.operands)),
+        in_specs=[ANY] + [VMEM] * 4 + [ANY] * len(work.operands),
         out_specs=[VMEM] * 2 + [ANY] * len(work.columns),
         scratch_shapes=collect_shapes(size)
         + [
@@ -791,7 +804,7 @@
 
 
 def feedforward_kernel(core, rows, upstream, weights, *refs):
-    before, refs = refs[:-5], refs[-5:]
+    before, refs = refs[:-5][:2], refs[-5:]
     gate_out, up_out, hidden_out, back_out, down_out = refs
     weight = weights.at[0]
     size = gate_out.shape[1]
@@ -822,12 +835,12 @@
         down_out[:, across] = down.astype(low)
 
 
-def feedforward(core, rows, upstream, weights, before=()):
+def feedforward(core, rows, upstream, weights, start, hidden, before=()):
     count = rows.shape[0]
-    hidden = weights.shape[2] // 3
-
-    def block(columns):
-        return pl.BlockSpec((FEEDFORWARD_ROWS, columns), lambda index, core: (index, 0))
+    size = weights.shape[2] // 3
+
+    def block(columns, place=0):
+        return pl.BlockSpec((FEEDFORWARD_ROWS, columns), lambda index, core: (index, place))
 
     return pl.pallas_call(
         feedforward_kernel,
@@ -843,16 +856,18 @@
                     pipeline_mode=pl.Buffered(1),
                 ),
             ]
-            + [block(MODEL_WIDTH)] * len(before),
-            out_specs=[block(hidden)] * 3 + [block(MODEL_WIDTH)] * 2,
+            + [block(MODEL_WIDTH)] * len(before[:2])
+            + [ANY] * len(before[2:]),
+            out_specs=[block(size, start // size)] * 3 + [block(MODEL_WIDTH)] * 2,
         ),
         out_shape=[jax.ShapeDtypeStruct((count, hidden), low)] * 3
         + [jax.ShapeDtypeStruct((count, MODEL_WIDTH), low)] * 2,
+        input_output_aliases={6 + i: i for i in range(len(before[2:]))},
         compiler_params=pltpu.CompilerParams(vmem_limit_bytes=52 * 2**20),
         cost_estimate=pl.CostEstimate(
-            flops=12 * count * MODEL_WIDTH * hidden,
+            flops=12 * count * MODEL_WIDTH * size,
             bytes_accessed=48 * 2**20,
-            transcendentals=count * hidden,
+            transcendentals=count * size,
         ),
         name="feedforward_more" if before else "feedforward",
     )(core, rows, upstream, weights, *before)
@@ -894,10 +909,15 @@
 QUERY_ROWS = 256
 
 
-def attention_forward_kernel(groups, share, valid, start, pre, gains, cosine, sine, gated):
+def attention_forward_kernel(
+    groups, share, valid, start, rows_in, weights, gains, cosine, sine, pre, gated, partial
+):
     sequence = pl.program_id(0)
     heads = groups * share
-    length = pre.shape[0]
+    length, projected = pre.shape
+    for column in range(0, projected, 3 * HEAD_WIDTH):
+        columns = slice(column, min(column + 3 * HEAD_WIDTH, projected))
+        pre[:, columns] = dot(rows_in[...], weights[:, columns], 1, 0)
     for group in range(groups):
         keys = head_rows(pre[:, head_at(heads + group)], gains[1:2, :], cosine[...], sine[...])
         values = pre[:, head_at(heads + groups + group)].astype(low)
@@ -911,14 +931,20 @@
                 mixed = dot(probs.astype(low), values, 1, 0)
                 gate = gate_column(pre[rows, head_at(heads + 2 * groups)], head)
                 gated[rows, head_at(head)] = (mixed * gate).astype(low)
+    for column in range(0, MODEL_WIDTH, 512):
+        partial[:, column : column + 512] = dot(
+            gated[...], weights[column : column + 512, projected:], 1, 1
+        ).astype(low)
 
 
 def attention_backward_kernel(
-    groups, share, valid, start, pre, upstream, gains, cosine, sine, grads, gain_grads
+    groups, share, valid, start, pre, rows_in, weights, gains, cosine, sine,
+    grads, gain_grads, partial, upstream,
 ):
     sequence = pl.program_id(0)
     heads = groups * share
-    length = pre.shape[0]
+    length, projected = pre.shape
+    upstream[...] = dot(rows_in[...], weights[:, projected:], 1, 0)
     scale = HEAD_WIDTH ** (-0.5)
 
     @pl.when(sequence == 0)
@@ -973,6 +999,10 @@
         grads[slice(at, at + QUERY_ROWS), head_at(heads + 2 * groups)] = logit_grads[block].astype(
             low
         )
+    for column in range(0, MODEL_WIDTH, 512):
+        partial[:, column : column + 512] = dot(
+            grads[...], weights[column : column + 512, :projected], 1, 1
+        ).astype(low)
 
 
 def sequence_block(columns, length):
@@ -986,62 +1016,83 @@
 SCALARS = pl.BlockSpec(memory_space=pltpu.SMEM)
 
 
-def attention_forward(groups, share, valid, start, pre, gains, cosine, sine):
+def attention_call(body, name, specs, sequences, outputs, out_specs, scratch, operands):
+    return pl.pallas_call(
+        body,
+        grid=(sequences,),
+        out_shape=outputs,
+        in_specs=[SCALARS, SCALARS, *specs],
+        out_specs=out_specs,
+        scratch_shapes=scratch,
+        compiler_params=pltpu.CompilerParams(vmem_limit_bytes=52 * 2**20),
+        cost_estimate=pl.CostEstimate(
+            flops=2**33, bytes_accessed=24 * 2**20, transcendentals=2**21
+        ),
+        name=name,
+    )(*operands)
+
+
+def attention_specs(weights, length):
+    return [
+        pl.BlockSpec(weights.shape, lambda sequence: (0, 0), pipeline_mode=pl.Buffered(1)),
+        fixed_block(2, HEAD_WIDTH),
+        fixed_block(length, HEAD_WIDTH),
+        fixed_block(length, HEAD_WIDTH),
+    ]
+
+
+def attention_forward(groups, share, valid, start, rows, weights, gains, cosine, sine):
     length, columns = cosine.shape[0], groups * share * HEAD_WIDTH
+    projected, count = weights.shape[1] - columns, rows.shape[0]
 
     def body(*refs):
         attention_forward_kernel(groups, share, *refs)
 
-    return pl.pallas_call(
+    return attention_call(
         body,
-        grid=(pre.shape[0] // length,),
-        out_shape=jax.ShapeDtypeStruct((pre.shape[0], columns), low),
-        in_specs=[
-            SCALARS,
-            SCALARS,
-            sequence_block(pre.shape[1], length),
-            fixed_block(2, HEAD_WIDTH),
-            fixed_block(length, HEAD_WIDTH),
-            fixed_block(length, HEAD_WIDTH),
+        "attention_forward",
+        [sequence_block(MODEL_WIDTH, length), *attention_specs(weights, length)],
+        count // length,
+        [
+            jax.ShapeDtypeStruct((count, projected), wide),
+            jax.ShapeDtypeStruct((count, columns), low),
+            jax.ShapeDtypeStruct((count, MODEL_WIDTH), low),
         ],
-        out_specs=sequence_block(columns, length),
-        compiler_params=pltpu.CompilerParams(vmem_limit_bytes=48 * 2**20),
-        cost_estimate=pl.CostEstimate(
-            flops=2**30, bytes_accessed=8 * 2**20, transcendentals=2**21
-        ),
-        name="attention_forward",
-    )(valid, start, pre, gains, cosine, sine)
-
-
-def attention_backward(groups, share, valid, start, pre, upstream, gains, cosine, sine):
-    length = cosine.shape[0]
+        [sequence_block(size, length) for size in (projected, columns, MODEL_WIDTH)],
+        [],
+        (valid, start, rows, weights, gains, cosine, sine),
+    )
+
+
+def attention_backward(groups, share, valid, start, pre, rows, weights, gains, cosine, sine):
+    length, columns = cosine.shape[0], groups * share * HEAD_WIDTH
+    count, projected = pre.shape
 
     def body(*refs):
         attention_backward_kernel(groups, share, *refs)
 
-    return pl.pallas_call(
+    return attention_call(
         body,
-        grid=(pre.shape[0] // length,),
-        out_shape=[
-            jax.ShapeDtypeStruct(pre.shape, low),
+        "attention_backward",
+        [
+            sequence_block(projected, length),
+            sequence_block(MODEL_WIDTH, length),
+            *attention_specs(weights, length),
+        ],
+        count // length,
+        [
+            jax.ShapeDtypeStruct((count, projected), low),
             jax.ShapeDtypeStruct((2, HEAD_WIDTH), wide),
+            jax.ShapeDtypeStruct((count, MODEL_WIDTH), low),
         ],
-        in_specs=[
-            SCALARS,
-            SCALARS,
-            sequence_block(pre.shape[1], length),
-            sequence_block(upstream.shape[1], length),
+        [
+            sequence_block(projected, length),
             fixed_block(2, HEAD_WIDTH),
-            fixed_block(length, HEAD_WIDTH),
-            fixed_block(length, HEAD_WIDTH),
+            sequence_block(MODEL_WIDTH, length),
         ],
-        out_specs=[sequence_block(pre.shape[1], length), fixed_block(2, HEAD_WIDTH)],
-        compiler_params=pltpu.CompilerParams(vmem_limit_bytes=48 * 2**20),
-        cost_estimate=pl.CostEstimate(
-            flops=2**32, bytes_accessed=12 * 2**20, transcendentals=2**21
-        ),
-        name="attention_backward",
-    )(valid, start, pre, upstream, gains, cosine, sine)
+        [pltpu.VMEM((length, columns), wide)],
+        (valid, start, pre, rows, weights, gains, cosine, sine),
+    )
 
 
 def adam_kernel(layouts, names, heads, *refs):
@@ -1228,29 +1279,39 @@
     large_both = lax.all_gather(large_block, ("w", "c"), axis=1, tiled=True)
     small_both = lax.all_gather(small_block, ("w", "c"), axis=1, tiled=True)
     attention_full, first_full, output_grad_full = gather_attention(mine, other, normed, cotangent)
-    projection_full, output_full = attention_full[:, : edges[4]], attention_full[:, edges[4] :]
     valid_pair = lax.dynamic_slice_in_dim(valid_len, 2 * group, 2)
     start_pair = lax.dynamic_slice_in_dim(pic_start, 2 * group, 2)
     cosine, sine = rotary_tables(length_value)
-    projected = dot(first_full, projection_full, 1, 0)
-    gated_low = attention_forward(
-        groups_here, share, valid_pair, start_pair, projected, head_gains, cosine, sine
-    )
-    attention_local, second_full = exchange_forward(
-        dot(gated_low, output_full, 1, 1).astype(low), tokens, norm_gains[1:2]
-    )
+    projected, gated_low, attention_partial = attention_forward(
+        groups_here,
+        share,
+        valid_pair,
+        start_pair,
+        first_full,
+        attention_full,
+        head_gains,
+        cosine,
+        sine,
+    )
+    attention_local, second_full = exchange_forward(attention_partial, tokens, norm_gains[1:2])
     middle = residual + attention_local
-    gate_large, up_large, hidden_large, *before = feedforward(
-        core[None], second_full, output_grad_full, large_both
-    )
-    gate_small, up_small, hidden_small, second_partial, feedforward_partial = feedforward(
-        core[None], second_full, output_grad_full, small_both, before
+    *held, back_partial, down_partial = feedforward(
+        core[None], second_full, output_grad_full, large_both, 0, hidden_here
+    )
+    gate_grad, up_grad, hidden_low, second_partial, feedforward_partial = feedforward(
+        core[None],
+        second_full,
+        output_grad_full,
+        small_both,
+        sizes[0],
+        hidden_here,
+        (back_partial, down_partial, *held),
     )
     own_places = place * local_rows + jnp.arange(local_rows, dtype=jnp.int32)
     counted = (own_places < valid_pair[core]).astype(wide)[:, None]
-    half = sizes[0] // 2
-    pieces = [(0, half), (half, sizes[0] - half)]
-    middle_grad, second_gain_grad, feedforward_local, output_squares, attention_grad, *sums = (
+    half = hidden_here // 2
+    pieces = [(0, half), (half, hidden_here - half)]
+    middle_grad, second_gain_grad, block_output, output_squares, attention_grad, *sums = (
         exchange_backward(
             second_partial,
             feedforward_partial,
@@ -1258,25 +1319,21 @@
             cotangent,
             norm_gains[1:2],
             counted,
-            [
-                (second_full, grad, *piece) for grad in (gate_large, up_large) for piece in pieces
-            ]
-            + [(second_full, grad, 0, sizes[1]) for grad in (gate_small, up_small)],
+            [(second_full, grad, *piece) for grad in (gate_grad, up_grad) for piece in pieces],
         )
     )
-    block_output = (middle + feedforward_local).astype(low)
-    projected_grad, head_gain_grads = attention_backward(
+    projected_grad, head_gain_grads, first_partial = attention_backward(
         groups_here,
         share,
         valid_pair,
         start_pair,
         projected,
-        dot(attention_grad, output_full, 1, 0),
+        attention_grad,
+        attention_full,
         head_gains,
         cosine,
         sine,
     )
-    first_partial = dot(projected_grad, projection_full, 1, 1)
     squares = jnp.stack(
         [
             jnp.sum(counted * residual * residual),
@@ -1294,25 +1351,24 @@
             jnp.tile(nothing, (4, 1)),
         ]
     )
-    tokens_grad, stats, projected_sums, output_sums, *more = exchange_last(
-        first_partial.astype(low),
+    tokens_grad, stats, *more = exchange_last(
+        first_partial,
         tokens,
         norm_gains[0:1],
         middle_grad,
         stats,
         [
+            *((output_grad_full, hidden_low, *piece) for piece in pieces),
             (first_full, projected_grad, 0, edges[4]),
             (attention_grad, gated_low, 0, head_cols),
-        ]
-        + [(output_grad_full, hidden_large, *piece) for piece in pieces]
-        + [(output_grad_full, hidden_small, 0, sizes[1])],
+        ],
     )
     denominator = jnp.sum(valid_len).astype(wide) * MODEL_WIDTH
     inverse = jnp.full((1, HEAD_WIDTH), 1.0 / denominator)
     input_rate = MODEL_WIDTH ** (-0.5)
     down_rate = FF ** (-0.5)
     output_rate = max(QUERY_HEADS * HEAD_WIDTH // 128, 4) ** (-0.5)
-    widths = [half, sizes[0] - half, sizes[1]]
+    widths = [half, hidden_here - half]
 
     def parts_of(name):
         return [(f"{name} {index}", 0, width) for index, width in enumerate(widths)]
@@ -1332,9 +1388,8 @@
         ),
         (True, output_rate, [[("output", 0, head_cols)]]),
     ]
-    names = ["gate 0", "gate 1", "up 0", "up 1", "gate 2", "up 2", "down 0", "down 1", "down 2"]
+    names = ["gate 0", "gate 1", "up 0", "up 1", "down 0", "down 1", "projected", "output"]
     sums = dict(zip(names, [*sums, *more]))
-    sums["projected"], sums["output"] = projected_sums, output_sums
     scales, *updated = adam_matrices(
         layouts,
         (edges[3], heads_here),

time: 715 us -> 685 us (0.958)
  matrix products: 29.7 us -> 0 us
    dot_general x4 -> x0, matrix products: 29.7 us -> none  [dot(): lax.dot_general(left, right, (((left_dim,), (right_dim,)), ((), ())), pre...]
    pallas_call x2, Pallas kernels: 35.5 us -> 57.5 us  [attention_call(): pl.pallas_call(body, grid=(sequences,), out_shape=outputs, in_specs=[SCAL...]
    pallas_call x1, Pallas kernels: 155 us -> 135 us  [exchange_backward(): pl.pallas_call(body, out_shape=[jax.ShapeDtypeStruct((size, MODEL_WIDTH),...]
  transfers between devices with their start and end apart: 2 -> 2, of which waited for: 1 -> 1; matrix products, arithmetic and copies ran while one was open for 4% -> 1% of each run, Pallas kernels for 37% -> 40%
where the time goes in v1:
time: 685 us; the launch traced here: 681 us
  Pallas kernels  615 us (90%)
  local copies, waits for them, and re-layouts  24.7 us (4%)
  between operations  15.6 us (2%)
  other arithmetic  15.1 us (2%)
  waiting for transfers between devices  10.4 us (2%)
    pallas_call x1, Pallas kernels, gather_attention(): pl.pallas_call(gather_kernel, out_shape=[jax.ShapeDtypeStruct((MODEL_WIDT...  150 us
    pallas_call x1, Pallas kernels, exchange_last(): pl.pallas_call(body, out_shape=[jax.ShapeDtypeStruct((size, MODEL_WIDTH),...  144 us
    pallas_call x1, Pallas kernels, exchange_backward(): pl.pallas_call(body, out_shape=[jax.ShapeDtypeStruct((size, MODEL_WIDTH),...  135 us
    pallas_call x2, Pallas kernels, feedforward(): pl.pallas_call(feedforward_kernel, grid_spec=pltpu.PrefetchScalarGridSpec...  58.2 us
    pallas_call x2, Pallas kernels, attention_call(): pl.pallas_call(body, grid=(sequences,), out_shape=outputs, in_specs=[SCAL...  57.5 us
    pallas_call x1, Pallas kernels, exchange_forward(): pl.pallas_call(forward_kernel, out_shape=[jax.ShapeDtypeStruct((size, MOD...  55.1 us
    pallas_call x1, Pallas kernels, adam_matrices(): pl.pallas_call(body, out_shape=like([inverse, *small, *states]), in_specs...  15.1 us
    unnamed x116, local copies, waits for them, and re-layouts  13.9 us
  transfers between devices with their start and end apart: 2, of which 1 were waited for; matrix products, arithmetic and copies ran while one was open for 1% of the time, Pallas kernels for 40%

profile of v1, /device:TPU:0, one launch (start us, length us, event | category | flops | bytes accessed | tf_op | source)
XLA Modules:
  0.0 681.4 jit_solution(2323276153945526856)
XLA Ops:
  7.3 2.1 fusion.5
  9.4 0.9 fusion.16
  10.2 0.9 fusion.17
  12.1 0.9 fusion.18
  15.1 0.8 copy.67.refs_16_
  16.6 0.8 copy.68
  17.5 1.3 dynamic_slice.14
  19.5 1.3 fusion.4
  21.4 1.3 fusion.3.first
  23.0 1.4 pad_maximum_fusion
  25.5 1.0 broadcast_select_fusion
  29.0 149.8 %gather_attention.1 = (bf16[2048,1664]{1,0:T(8,128)(2,1)}, bf16[1024,2048]{1,0:T(8,128)(2,1)}, bf16[1024,2048]{1,0:T(8,128)(2,1)}) custom-call(bf16[128,1664]{1,0:T(8,128)(2,1)} %get-tuple-element.93.mine, bf16[128,1664]{1,0:T(8,128)(2,1)} %get-tuple-element.94.other, bf16[256,2048]{1,0:T(8,128)(2,1)} %fusion.3.first, bf16[256,2048]{1,0:T(8,128)(2,1)} %refs_3_.1), custom_call_target="tpu_custom_call" | custom-call | bytes 67108864 | tf_op jit(solution)/shard_map/gather_attention/pallas_call | solution.py:523
  178.8 1.0 fusion.12
  180.0 22.2 %attention_forward.1 = (f32[1024,1152]{1,0:T(8,128)}, bf16[1024,512]{1,0:T(8,128)(2,1)S(1)}, bf16[1024,2048]{1,0:T(8,128)(2,1)}) custom-call(s32[2]{0:T(128)S(1)} %dynamic_slice.11.refs_0_, s32[2]{0:T(128)S(1)} %dynamic_slice.12.refs_1_, bf16[1024,2048]{1,0:T(8,128)(2,1)} %get-tuple-element.96.refs_2_.refs_7_, ...), custom_call_target="tpu_custom_call" | custom-call | flops 8589934592 | bytes 25165824 | tf_op jit(solution)/shard_map/attention_forward/pallas_call | solution.py:1020
  202.3 1.0 copy-done.2
  203.3 55.1 %exchange_forward.1 = (f32[256,2048]{1,0:T(8,128)}, bf16[1024,2048]{1,0:T(8,128)(2,1)}) custom-call(bf16[1024,2048]{1,0:T(8,128)(2,1)} %get-tuple-element.98.partial, bf16[256,2048]{1,0:T(8,128)(2,1)} %refs_1_.1, f32[1,2048]{1,0:T(1,128)} %get-tuple-element.245.gain.refs_4_), custom_call_target="tpu_custom_call" | custom-call | bytes 67108864 | tf_op jit(solution)/shard_map/exchange_forward/pallas_call | solution.py:566
  258.4 1.3 fusion.11.refs_5_
  259.7 3.8 fusion
  263.5 42.9 %feedforward.1 = (bf16[1024,1536]{1,0:T(8,128)(2,1)}, bf16[1024,1536]{1,0:T(8,128)(2,1)}, bf16[1024,1536]{1,0:T(8,128)(2,1)}, bf16[1024,2048]{1,0:T(8,128)(2,1)}, bf16[1024,2048]{1,0:T(8,128)(2,1)}) custom-call(s32[1]{0:T(128)} %bitcast.core, bf16[1024,2048]{1,0:T(8,128)(2,1)} %get-tuple-element.99.rows.refs_6_, ...), custom_call_target="tpu_custom_call" | custom-call | flops 32212254720 | bytes 50331648 | tf_op jit(solution)/shard_map/feedforward/pallas_call | solution.py:845
  306.4 9.9 %all-gather.3.cloned.1.call-done.weights = bf16[2,2048,768]{2,1,0:T(8,128)(2,1)} async-done(((bf16[2,128,768]{2,1,0:T(8,128)(2,1)}), bf16[2,2048,768]{2,1,0:T(8,128)(2,1)}) %all-gather.3.cloned.1.call-update) | async-done | bytes 6291472 | tf_op jit(solution)/shard_map/all_gather | solution.py:1280
  316.3 15.4 %feedforward_more.1 = (bf16[1024,1536]{1,0:T(8,128)(2,1)}, bf16[1024,1536]{1,0:T(8,128)(2,1)}, bf16[1024,1536]{1,0:T(8,128)(2,1)}, bf16[1024,2048]{1,0:T(8,128)(2,1)}, bf16[1024,2048]{1,0:T(8,128)(2,1)}) custom-call(s32[1]{0:T(128)} %bitcast.core, ...), custom_call_target="tpu_custom_call", output_to_operand_aliasing={{0}: (6, {}), {1}: (7, {}), {2}: (8, {})} | custom-call | flops 6442450944 | bytes 50331648 | tf_op jit(solution)/shard_map/feedforward_more/pallas_call | solution.py:845
  331.7 135.3 %exchange_backward.1 = (f32[256,2048]{1,0:T(8,128)}, f32[1,2048]{1,0:T(1,128)}, bf16[256,2048]{1,0:T(8,128)(2,1)}, f32[1,2048]{1,0:T(1,128)}, bf16[1024,2048]{1,...) custom-call(bf16[1024,2048]{1,0:T(8,128)(2,1)} %get-tuple-element.10, ...), custom_call_target="tpu_custom_call" | custom-call | bytes 134217728 | tf_op jit(solution)/shard_map/exchange_backward/pallas_call | solution.py:668
  467.1 35.3 %attention_backward.1 = (bf16[1024,1152]{1,0:T(8,128)(2,1)}, f32[2,128]{1,0:T(2,128)S(1)}, bf16[1024,2048]{1,0:T(8,128)(2,1)}) custom-call(s32[2]{0:T(128)S(1)} %dynamic_slice.11.refs_0_, s32[2]{0:T(128)S(1)} %dynamic_slice.12.refs_1_, f32[1024,1152]{1,0:T(8,128)} %get-tuple-element.114.refs_2_, bf16[1024,2048]{1,0:T(8,128)(2,1)} %get-tuple-element.115.refs_3_.refs_9_, ...), custom_call_target="tpu_custom_call" | custom-call | flops 8589934592 | bytes 25165824 | tf_op jit(solution)/shard_map/attention_backward/pallas_call | solution.py:1020
  502.3 1.4 select_maximum_fusion
  504.5 144.2 %exchange_last.1 = (f32[256,2048]{1,0:T(8,128)}, f32[8,2048]{1,0:T(8,128)}, bf16[2,128,768]{2,1,0:T(8,128)(2,1)}, bf16[2,128,768]{2,1,0:T(8,128)(2,1)}, bf16[2,1...) custom-call(bf16[1024,2048]{1,0:T(8,128)(2,1)} %get-tuple-element.116.refs_0_, bf16[256,2048]{1,0:T(8,128)(2,1)} %refs_1_.1, ...), custom_call_target="tpu_custom_call" | custom-call | bytes 134217728 | tf_op jit(solution)/shard_map/exchange_last/pallas_call | solution.py:779
  648.8 1.0 copy-done.10
  649.8 1.0 copy-done.11
  650.8 0.9 copy-done.12
  651.7 0.8 copy-done.13
  652.6 15.1 %adam_matrices.1 = (f32[1,128]{1,0:T(1,128)S(1)}, f32[2,2048]{1,0:T(2,128)}, f32[2,2048]{1,0:T(2,128)}, f32[2,2048]{1,0:T(2,128)}, f32[2,128]{1,0:T(2,128)}, /*i...) custom-call(bf16[2,128,768]{2,1,0:T(8,128)(2,1)S(1)} %copy-done.6, ...), custom_call_target="tpu_custom_call" | custom-call | flops 33554432 | bytes 41943040 | tf_op jit(solution)/shard_map/adam_matrices/pallas_call | solution.py:1181
  670.2 1.0 copy.90
  671.2 3.1 copy.91
  (136 shorter events, 11.6 us)
Async XLA Ops:
  7.2 256.3 %all-gather.5.cloned.1.call-start = ((), (), s32[]{:S(2)}) async-start(), calls=%async_computation.1 | async-start | bytes 33423360 | tf_op jit(solution)/shard_map/all_gather | solution.py:1279
  11.8 2.6 copy-start.1
  12.1 7.4 %copy-start.20 = (bf16[256,2048]{1,0:T(8,128)(2,1)S(1)}, bf16[256,2048]{1,0:T(8,128)(2,1)}, u32[]{:S(2)}) copy-start(bf16[256,2048]{1,0:T(8,128)(2,1)} %refs_1_.1) | copy-start | bytes 3145732
  13.0 7.8 %copy-start.14 = (f32[2,2048]{1,0:T(2,128)S(1)}, f32[2,2048]{1,0:T(2,128)}, u32[]{:S(2)}) copy-start(f32[2,2048]{1,0:T(2,128)} %refs_10_.1) | copy-start | bytes 49156
  13.6 3.0 copy-start.23
  15.9 6.8 %copy-start.24 = (bf16[128,1280]{1,0:T(8,128)(2,1)S(1)}, bf16[128,1280]{1,0:T(8,128)(2,1)}, u32[]{:S(2)}) copy-start(bf16[128,1280]{1,0:T(8,128)(2,1)} %get-tuple-element.227) | copy-start | bytes 983044
  15.9 6.8 %copy-start.25 = (bf16[128,1280]{1,0:T(8,128)(2,1)S(1)}, bf16[128,1280]{1,0:T(8,128)(2,1)}, u32[]{:S(2)}) copy-start(bf16[128,1280]{1,0:T(8,128)(2,1)} %get-tuple-element.228) | copy-start | bytes 983044
  17.4 5.3 copy-start.26
  18.7 4.0 copy-start.27
  18.7 4.0 copy-start.28
  18.7 4.0 copy-start.29
  25.5 2.5 copy-start.50
  25.5 2.6 copy-start.47
  25.5 2.7 copy-start.48
  26.5 289.8 %all-gather.3.cloned.1.call-start = ((), (), s32[]{:S(2)}) async-start(), calls=%async_computation | async-start | bytes 6684672 | tf_op jit(solution)/shard_map/all_gather | solution.py:1280
  29.0 151.1 %copy-start.17 = (f32[2,128]{1,0:T(2,128)S(1)}, f32[2,128]{1,0:T(2,128)}, u32[]{:S(2)}) copy-start(f32[2,128]{1,0:T(2,128)} %refs_13_.1) | copy-start | bytes 3076
  203.2 56.5 %copy-start.21 = (bf16[256,2048]{1,0:T(8,128)(2,1)S(1)}, bf16[256,2048]{1,0:T(8,128)(2,1)}, u32[]{:S(2)}) copy-start(bf16[256,2048]{1,0:T(8,128)(2,1)} %refs_1_.1) | copy-start | bytes 3145732
  203.3 56.5 %copy-start.44 = (f32[256]{0:T(256)S(1)}, f32[256]{0:T(256)}, u32[]{:S(2)}) copy-start(f32[256]{0:T(256)} %copy-done.43) | copy-start | bytes 3076
  467.0 36.7 %copy-start.45 = (f32[1,2048]{1,0:T(1,128)S(1)}, f32[1,2048]{1,0:T(1,128)}, u32[]{:S(2)}) copy-start(f32[1,2048]{1,0:T(1,128)} %get-tuple-element.118) | copy-start | bytes 24580
  467.1 36.7 %copy-start.46 = (f32[1,2048]{1,0:T(1,128)S(1)}, f32[1,2048]{1,0:T(1,128)}, u32[]{:S(2)}) copy-start(f32[1,2048]{1,0:T(1,128)} %get-tuple-element.120) | copy-start | bytes 24580
  504.4 144.3 %copy-start.3 = (f32[128,1024]{1,0:T(8,128)S(1)}, f32[128,1024]{1,0:T(8,128)}, u32[]{:S(2)}) copy-start(f32[128,1024]{1,0:T(8,128)} %refs_26_.1) | copy-start | bytes 1572868
  504.4 144.3 %copy-start.4 = (f32[128,1024]{1,0:T(8,128)S(1)}, f32[128,1024]{1,0:T(8,128)}, u32[]{:S(2)}) copy-start(f32[128,1024]{1,0:T(8,128)} %refs_27_.1) | copy-start | bytes 1572868
  504.4 144.3 %copy-start.5 = (f32[2,128,512]{2,1,0:T(8,128)S(1)}, f32[2,128,512]{2,1,0:T(8,128)}, u32[]{:S(2)}) copy-start(f32[2,128,512]{2,1,0:T(8,128)} %refs_29_.1) | copy-start | bytes 1572868
  504.4 144.3 %copy-start.6 = (bf16[2,128,768]{2,1,0:T(8,128)(2,1)S(1)}, bf16[2,128,768]{2,1,0:T(8,128)(2,1)}, u32[]{:S(2)}) copy-start(bf16[2,128,768]{2,1,0:T(8,128)(2,1)} %get-tuple-element.125.refs_0_) | copy-start | bytes 1179652
  504.4 144.3 %copy-start.7 = (bf16[2,128,768]{2,1,0:T(8,128)(2,1)S(1)}, bf16[2,128,768]{2,1,0:T(8,128)(2,1)}, u32[]{:S(2)}) copy-start(bf16[2,128,768]{2,1,0:T(8,128)(2,1)} %get-tuple-element.126.refs_1_) | copy-start | bytes 1179652
  504.4 144.3 %copy-start.8 = (bf16[2,128,768]{2,1,0:T(8,128)(2,1)S(1)}, bf16[2,128,768]{2,1,0:T(8,128)(2,1)}, u32[]{:S(2)}) copy-start(bf16[2,128,768]{2,1,0:T(8,128)(2,1)} %get-tuple-element.127.refs_2_) | copy-start | bytes 1179652
  504.5 144.3 %copy-start.9 = (bf16[2,128,768]{2,1,0:T(8,128)(2,1)S(1)}, bf16[2,128,768]{2,1,0:T(8,128)(2,1)}, u32[]{:S(2)}) copy-start(bf16[2,128,768]{2,1,0:T(8,128)(2,1)} %get-tuple-element.128.refs_3_) | copy-start | bytes 1179652
  504.5 144.3 %copy-start.15 = (f32[2,2048]{1,0:T(2,128)S(1)}, f32[2,2048]{1,0:T(2,128)}, u32[]{:S(2)}) copy-start(f32[2,2048]{1,0:T(2,128)} %refs_11_.1) | copy-start | bytes 49156
  504.5 144.3 %copy-start.16 = (f32[2,2048]{1,0:T(2,128)S(1)}, f32[2,2048]{1,0:T(2,128)}, u32[]{:S(2)}) copy-start(f32[2,2048]{1,0:T(2,128)} %refs_12_.1) | copy-start | bytes 49156
  504.5 144.3 %copy-start.18 = (f32[2,128]{1,0:T(2,128)S(1)}, f32[2,128]{1,0:T(2,128)}, u32[]{:S(2)}) copy-start(f32[2,128]{1,0:T(2,128)} %refs_14_.1) | copy-start | bytes 3076
  504.5 144.3 %copy-start.19 = (f32[2,128]{1,0:T(2,128)S(1)}, f32[2,128]{1,0:T(2,128)}, u32[]{:S(2)}) copy-start(f32[2,128]{1,0:T(2,128)} %refs_15_.1) | copy-start | bytes 3076
  652.6 17.6 %copy-start.31 = (bf16[256,2048]{1,0:T(8,128)(2,1)S(1)}, bf16[256,2048]{1,0:T(8,128)(2,1)}, u32[]{:S(2)}) copy-start(bf16[256,2048]{1,0:T(8,128)(2,1)} %get-tuple-element.285) | copy-start | bytes 3145732
  (21 other events, 34.2 us)
Sparse Core Ops, SparseCore 0:
  26.7 224.7 all-gather.4
  254.3 61.9 all-gather.2
